TPU v7x, 512 devices: a whole 4x4x16 slice. The times are simulated.
512 devices in a mesh: row: 16 (over z), col: 32 (over y, x, core).
Axes of the slice: x: 4, y: 4, z: 16, core: 2. Of those that a mesh axis runs over, the one named last changes fastest.
Arguments:
- view_images: float32 [8, 3, 2048, 4096], P(None, None, 'row', 'col'), may hold values from -4 to 4
- intersection_bits: int32 [16, 32], P('row', 'col'), may hold values from 1 to 255
- seam_labels: int32 [16, 32], P('row', 'col'), may hold values from 0 to 7
Outputs:
- panorama: float32 [3, 2048, 4096], P(None, 'row', 'col')
All inputs are finite; a program needn't handle non-finite values.
Results may differ from a plain program's by a relative error of at most 0.0001.
Values sent between devices are 32-bit elements; how exact they have to be, the bound alone decides.
A program may use at most 128 MiB of HBM per device.

v0:
```python
import jax
import jax.numpy as jnp
from jax import lax
from jax.sharding import PartitionSpec as P

V = 8
C = 3
LEVELS = 8
BLOCK = 128


BINOMIAL = (1.0, 4.0, 6.0, 4.0, 1.0)


def padded(array, sides, width):
    for axis, dim in sides:
        peers, length = (lax.axis_size(axis), array.shape[dim])
        up = [(i, (i + 1) % peers) for i in range(peers - 1)]
        down = [(j, i) for i, j in up]
        last = lax.slice_in_dim(array, length - width, length, axis=dim)
        first = lax.slice_in_dim(array, 0, width, axis=dim)
        before = lax.ppermute(last, axis, up)
        after = lax.ppermute(first, axis, down)
        array = jnp.concatenate([before, array, after], axis=dim)
    return array


def border(field, rim_width):
    return jnp.pad(field, ((0, 0), (rim_width, rim_width), (rim_width, rim_width)))


def shrink_axis(padded_in, rim_width, margin, along_axis):
    out_len = (padded_in.shape[along_axis] - 2 * rim_width) // 2 + 2 * margin
    accumulated = None
    for tap_index in range(5):
        begin = rim_width - 2 * margin + tap_index - 2
        sliced = lax.slice_in_dim(padded_in, begin, begin + 2 * out_len - 1, 2, along_axis)
        weighted = BINOMIAL[tap_index] * sliced
        accumulated = weighted if accumulated is None else accumulated + weighted
    return accumulated / 16.0


def spread_axis(coarse_pad, along_axis):
    out_len = coarse_pad.shape[along_axis] - 2
    below_cells = lax.slice_in_dim(coarse_pad, 0, out_len, 1, along_axis)
    centre_cells = lax.slice_in_dim(coarse_pad, 1, out_len + 1, 1, along_axis)
    above_cells = lax.slice_in_dim(coarse_pad, 2, out_len + 2, 1, along_axis)
    even_part = (below_cells + 6.0 * centre_cells + above_cells) / 8.0
    odd_part = (centre_cells + above_cells) / 2.0
    paired = jnp.stack([even_part, odd_part], axis=along_axis + 1)
    out_shape = list(even_part.shape)
    out_shape[along_axis] = 2 * out_len
    return paired.reshape(out_shape)


def reduce_both(padded_in, rim_width, margin):
    return shrink_axis(shrink_axis(padded_in, rim_width, margin, 1), rim_width, margin, 2)


def expand_both(coarse_pad):
    return spread_axis(spread_axis(coarse_pad, 1), 2)


def masks_from(intersection_bits, seam_labels):
    view_ids = jnp.arange(V, dtype=jnp.int32)[:, None, None]
    view_bits = jnp.bitwise_and(jnp.right_shift(intersection_bits[None], view_ids), 1).astype(
        jnp.float32
    )
    chosen = (seam_labels[None] == view_ids).astype(jnp.float32)
    block_masks = view_bits * (1.0 + 3.0 * chosen)
    return jnp.repeat(jnp.repeat(block_masks, BLOCK, axis=1), BLOCK, axis=2)


def blend_level(detail, view_masks):
    weight_sum = jnp.sum(view_masks, axis=0)
    shares = view_masks / weight_sum
    layered = detail.reshape(V, C, detail.shape[1], detail.shape[2])
    return jnp.sum(shares[:, None] * layered, axis=0)


def compensate(top_images):
    layered = top_images.reshape(V, C, top_images.shape[1], top_images.shape[2])
    view_means = jnp.mean(layered, axis=(2, 3), keepdims=True)
    common_mean = jnp.mean(view_means, axis=0, keepdims=True)
    return (layered - view_means + common_mean).reshape(top_images.shape)


def collapse(images, view_masks, steps_down):
    level_index = 0
    coarser = reduce_both(border(images, 2), 2, 0)
    coarse_masks = reduce_both(border(view_masks, 2), 2, 0)
    detail = images - expand_both(border(coarser, 1))
    blended = [blend_level(detail, view_masks)]
    result = blend_level(compensate(coarser), coarse_masks)
    for level_index in reversed(range(steps_down)):
        result = blended[level_index] + expand_both(border(result, 1))
    return result


def local_margin(full_field, rows_here, cols_here):
    padded_full = border(full_field, 1)
    row_start = lax.axis_index("row") * rows_here
    col_start = lax.axis_index("col") * cols_here
    sliced = lax.dynamic_slice_in_dim(padded_full, row_start, rows_here + 2, 1)
    return lax.dynamic_slice_in_dim(sliced, col_start, cols_here + 2, 2)


def edge_rims(planes_in):
    return padded(planes_in, (("row", 1), ("col", 2)), 2)


def padded_masks(intersection_bits, seam_labels, rim_width, rows_tile, cols_tile):
    stacked = jnp.stack([intersection_bits, seam_labels], axis=0)
    beside_all = padded(stacked, (("row", 1), ("col", 2)), 1)
    spread = masks_from(beside_all[0], beside_all[1])
    row_begin = BLOCK - rim_width
    return spread[
        :,
        row_begin : row_begin + rows_tile + 2 * rim_width,
        row_begin : row_begin + cols_tile + 2 * rim_width,
    ]


def local(view_images, intersection_bits, seam_labels):
    planes = V * C
    rows_tile = view_images.shape[2]
    cols_tile = view_images.shape[3]
    images = view_images.reshape(planes, rows_tile, cols_tile)
    rim_width = 2
    margin = 0
    fold_level = LEVELS - 2
    blended = []
    masks_here = None
    for level_index in range(fold_level):
        if level_index == 0:
            padded_img = edge_rims(images)
            padded_msk = padded_masks(
                intersection_bits, seam_labels, rim_width, rows_tile, cols_tile
            )
            reduced = jnp.concatenate(
                [
                    reduce_both(padded_img, rim_width, margin),
                    reduce_both(padded_msk, rim_width, margin),
                ],
                axis=0,
            )
            masks_here = padded_msk[:, rim_width:-rim_width, rim_width:-rim_width]
        else:
            padded_in = edge_rims(jnp.concatenate([images, masks_here], axis=0))
            reduced = reduce_both(padded_in, rim_width, margin)
        coarse_pad = None
        if level_index + 1 < fold_level:
            coarse_pad = padded(reduced[:planes], (("row", 1), ("col", 2)), 1)
        if level_index + 1 < fold_level:
            detail = images - expand_both(coarse_pad)
            blended.append(blend_level(detail, masks_here))
        else:
            finest_images = images
            finest_masks = masks_here
        images = reduced[:planes]
        masks_here = reduced[planes:]
    planes_all = jnp.concatenate([images, masks_here], axis=0)
    rows_here = planes_all.shape[1]
    cols_here = planes_all.shape[2]
    gathered = lax.all_gather(planes_all, "col", axis=2, tiled=True)
    gathered = lax.all_gather(gathered, "row", axis=1, tiled=True)
    top = collapse(gathered[:planes], gathered[planes:], LEVELS - 1 - fold_level)
    detail = finest_images - expand_both(local_margin(gathered[:planes], rows_here, cols_here))
    result = blend_level(detail, finest_masks) + expand_both(
        local_margin(top, rows_here, cols_here)
    )
    for level_index in reversed(range(fold_level - 1)):
        rimmed = padded(result, (("row", 1), ("col", 2)), 1)
        result = blended[level_index] + expand_both(rimmed)
    return result


def solution(mesh):
    placed = (P(None, None, "row", "col"), P("row", "col"), P("row", "col"))
    return jax.shard_map(
        local, mesh=mesh, in_specs=placed, out_specs=P(None, "row", "col"), check_vma=False
    )
```

profile of v0, /device:TPU:112, one launch (start us, length us, event | category | flops | bytes accessed | tf_op | source)
XLA Modules:
  0.0 625.4 jit_solution(9791726391585337434)
XLA Ops:
  34.8 9.4 %slice.813 = f32[8,64,132]{1,2,0:T(8,128)S(1)} slice(f32[8,132,132]{1,2,0:T(8,128)S(1)} %slice.1050), slice={[0:8:1], [4:131:2], [0:132:1]} | slice | bytes 540672 | tf_op jit(solution)/shard_map/slice | solution.py:37
  44.1 9.4 %slice.812 = f32[8,64,132]{1,2,0:T(8,128)S(1)} slice(f32[8,132,132]{1,2,0:T(8,128)S(1)} %slice.1050), slice={[0:8:1], [3:130:2], [0:132:1]} | slice | bytes 540672 | tf_op jit(solution)/shard_map/slice | solution.py:37
  53.5 10.0 %slice.811 = f32[8,64,132]{1,2,0:T(8,128)} slice(f32[8,132,132]{1,2,0:T(8,128)S(1)} %slice.1050), slice={[0:8:1], [2:129:2], [0:132:1]} | slice | bytes 540672 | tf_op jit(solution)/shard_map/slice | solution.py:37
  63.5 9.8 %slice.809 = f32[8,64,132]{1,2,0:T(8,128)} slice(f32[8,132,132]{1,2,0:T(8,128)S(1)} %slice.1050), slice={[0:8:1], [0:127:2], [0:132:1]} | slice | bytes 540672 | tf_op jit(solution)/shard_map/slice | solution.py:37
  73.2 9.9 %slice.810 = f32[8,64,132]{1,2,0:T(8,128)} slice(f32[8,132,132]{1,2,0:T(8,128)S(1)} %slice.1050), slice={[0:8:1], [1:128:2], [0:132:1]} | slice | bytes 540672 | tf_op jit(solution)/shard_map/slice | solution.py:37
  132.0 13.6 %slice.797 = f32[24,64,64]{2,1,0:T(8,128)S(1)} slice(f32[24,64,132]{2,1,0:T(8,128)S(1)} %add_multiply_fusion), slice={[0:24:1], [0:64:1], [4:131:2]} | slice | bytes 786432 | tf_op jit(solution)/shard_map/slice | solution.py:37
  145.7 13.6 %slice.796 = f32[24,64,64]{2,1,0:T(8,128)S(1)} slice(f32[24,64,132]{2,1,0:T(8,128)S(1)} %add_multiply_fusion), slice={[0:24:1], [0:64:1], [3:130:2]} | slice | bytes 786432 | tf_op jit(solution)/shard_map/slice | solution.py:37
  159.3 14.2 %slice.795 = f32[24,64,64]{2,1,0:T(8,128)} slice(f32[24,64,132]{2,1,0:T(8,128)S(1)} %add_multiply_fusion), slice={[0:24:1], [0:64:1], [2:129:2]} | slice | bytes 786432 | tf_op jit(solution)/shard_map/slice | solution.py:37
  173.4 13.9 %slice.793 = f32[24,64,64]{2,1,0:T(8,128)} slice(f32[24,64,132]{2,1,0:T(8,128)S(1)} %add_multiply_fusion), slice={[0:24:1], [0:64:1], [0:127:2]} | slice | bytes 786432 | tf_op jit(solution)/shard_map/slice | solution.py:37
  187.3 14.1 %slice.794 = f32[24,64,64]{2,1,0:T(8,128)} slice(f32[24,64,132]{2,1,0:T(8,128)S(1)} %add_multiply_fusion), slice={[0:24:1], [0:64:1], [1:128:2]} | slice | bytes 786432 | tf_op jit(solution)/shard_map/slice | solution.py:37
  220.6 5.3 collective-permute-start.12
  259.2 5.5 slice.832
  264.7 5.5 slice.831
  270.3 5.5 slice.830
  275.8 5.4 slice.828
  281.2 6.0 slice.829
  338.6 5.9 collective-permute-done.30
  349.9 5.4 collective-permute-start.36
  399.3 22.7 %all_gather.6 = f32[32,2,64]{0,1,2:T(2,128)S(1)} all-gather(f32[32,2,2]{0,1,2:T(2,128)S(1)} %copy.331), channel_id=1, replica_groups=mesh['row'=16,'col'=32] {'col'}, dimensions={2}, use_global_device_ids=true | all-gather | bytes 16896 | tf_op jit(solution)/shard_map/all_gather | solution.py:165
  422.1 31.5 %all_gather.7 = f32[32,32,64]{2,0,1:T(8,128)S(1)} all-gather(f32[32,2,64]{2,0,1:T(8,128)S(1)} %copy.332), channel_id=1, replica_groups=mesh['row'=16,'col'=32] {'row'}, dimensions={1}, use_global_device_ids=true | all-gather | bytes 278528 | tf_op jit(solution)/shard_map/all_gather | solution.py:166
  549.8 5.8 collective-permute-start.27
  559.8 5.9 collective-permute-done.26
  593.5 5.6 collective-permute-done.18
  605.3 5.4 collective-permute-start.64
  (481 shorter events, 382.2 us)
Async XLA Ops:
  1.3 18.7 %collective-permute-start.1 = (s32[2,1,1]{1,0,2:T(2,128)S(1)}, s32[2,1,1]{1,0,2:T(2,128)S(1)}, u32[]{:S(2)}, u32[]{:S(2)}) collective-permute-start(s32[2,1,1]{1,0,2:T(2,128)S(1)} %pad_add_fusion.1), channel_id=1, source_target_pairs={{32,0},{64,32},{96,64},{128,96},{160,128},{192,160},{224,192},{256... | collective-permute-start | bytes 32 | tf_op jit(solution)/shard_map/ppermute | solution.py:23
  3.3 16.7 %collective-permute-start = (s32[2,1,1]{1,0,2:T(2,128)S(1)}, s32[2,1,1]{1,0,2:T(2,128)S(1)}, u32[]{:S(2)}, u32[]{:S(2)}) collective-permute-start(s32[2,1,1]{1,0,2:T(2,128)S(1)} %pad_add_fusion.1), channel_id=1, source_target_pairs={{0,32},{32,64},{64,96},{96,128},{128,160},{160,192},{192,224},{224... | collective-permute-start | bytes 32 | tf_op jit(solution)/shard_map/ppermute | solution.py:22
  10.0 77.4 %collective-permute-start.5 = (f32[24,2,128]{2,1,0:T(2,128)}, f32[24,2,128]{2,1,0:T(2,128)S(1)}, u32[]{:S(2)}, u32[]{:S(2)}) collective-permute-start(f32[24,2,128]{2,1,0:T(2,128)} %get-tuple-element.16), channel_id=1, source_target_pairs={{32,0},{64,32},{96,64},{128,96},{160,128},{192,160},{224,192},{256... | collective-permute-start | bytes 73736 | tf_op jit(solution)/shard_map/ppermute | solution.py:23
  11.9 75.5 %collective-permute-start.4 = (f32[24,2,128]{2,1,0:T(2,128)S(1)}, f32[24,2,128]{2,1,0:T(2,128)S(1)}, u32[]{:S(2)}, u32[]{:S(2)}) collective-permute-start(f32[24,2,128]{2,1,0:T(2,128)S(1)} %get-tuple-element.15), channel_id=1, source_target_pairs={{0,32},{32,64},{64,96},{96,128},{128,160},{160,192},{192,224},{224... | collective-permute-start | bytes 73736 | tf_op jit(solution)/shard_map/ppermute | solution.py:22
  212.8 13.1 %collective-permute-start.11 = (f32[24,66,1]{1,0,2:T(8,128)S(1)}, f32[24,66,1]{1,0,2:T(8,128)S(1)}, u32[]{:S(2)}, u32[]{:S(2)}) collective-permute-start(f32[24,66,1]{1,0,2:T(8,128)S(1)} %copy.288), channel_id=1, source_target_pairs={{1,0},{2,1},{3,2},{4,3},{5,4},{6,5},{7,6},{8,7},{9,8},{10,9},{11,1... | collective-permute-start | bytes 19016 | tf_op jit(solution)/shard_map/ppermute | solution.py:23
  216.1 10.3 %collective-permute-start.10 = (f32[24,66,1]{1,0,2:T(8,128)S(1)}, f32[24,66,1]{1,0,2:T(8,128)S(1)}, u32[]{:S(2)}, u32[]{:S(2)}) collective-permute-start(f32[24,66,1]{1,0,2:T(8,128)S(1)} %copy.287), channel_id=1, source_target_pairs={{0,1},{1,2},{2,3},{3,4},{4,5},{5,6},{6,7},{7,8},{8,9},{9,10},{10,1... | collective-permute-start | bytes 19016 | tf_op jit(solution)/shard_map/ppermute | solution.py:22
  234.0 10.7 %collective-permute-start.15 = (f32[32,68,2]{1,0,2:T(8,128)}, f32[32,68,2]{1,0,2:T(8,128)}, u32[]{:S(2)}, u32[]{:S(2)}) collective-permute-start(f32[32,68,2]{1,0,2:T(8,128)} %copy.299), channel_id=1, source_target_pairs={{1,0},{2,1},{3,2},{4,3},{5,4},{6,5},{7,6},{8,7},{9,8},{10,9},{11,1... | collective-permute-start | bytes 52232 | tf_op jit(solution)/shard_map/ppermute | solution.py:23
  296.2 278.8 %collective-permute-start.17 = (f32[24,1,32]{2,1,0:T(1,128)}, f32[24,1,32]{2,1,0:T(1,128)}, u32[]{:S(2)}, u32[]{:S(2)}) collective-permute-start(f32[24,1,32]{2,1,0:T(1,128)} %get-tuple-element.38), channel_id=1, source_target_pairs={{32,0},{64,32},{96,64},{128,96},{160,128},{192,160},{224,192},{256... | collective-permute-start | bytes 9224 | tf_op jit(solution)/shard_map/ppermute | solution.py:23
  333.3 11.2 %collective-permute-start.30 = (f32[32,20,2]{2,1,0:T(8,128)S(1)}, f32[32,20,2]{2,1,0:T(8,128)S(1)}, u32[]{:S(2)}, u32[]{:S(2)}) collective-permute-start(f32[32,20,2]{2,1,0:T(8,128)S(1)} %get-tuple-element.47), channel_id=1, source_target_pairs={{0,1},{1,2},{2,3},{3,4},{4,5},{5,6},{6,7},{7,8},{8,9},{9,10},{10,1... | collective-permute-start | bytes 15368 | tf_op jit(solution)/shard_map/ppermute | solution.py:22
  347.9 14.6 %collective-permute-start.37 = (f32[32,2,8]{2,1,0:T(2,128)S(1)}, f32[32,2,8]{2,1,0:T(2,128)S(1)}, u32[]{:S(2)}, u32[]{:S(2)}) collective-permute-start(f32[32,2,8]{2,1,0:T(2,128)S(1)} %get-tuple-element.68), channel_id=1, source_target_pairs={{32,0},{64,32},{96,64},{128,96},{160,128},{192,160},{224,192},{256... | collective-permute-start | bytes 6152 | tf_op jit(solution)/shard_map/ppermute | solution.py:23
  349.9 12.7 %collective-permute-start.36 = (f32[32,2,8]{2,1,0:T(2,128)S(1)}, f32[32,2,8]{2,1,0:T(2,128)S(1)}, u32[]{:S(2)}, u32[]{:S(2)}) collective-permute-start(f32[32,2,8]{2,1,0:T(2,128)S(1)} %get-tuple-element.67), channel_id=1, source_target_pairs={{0,32},{32,64},{64,96},{96,128},{128,160},{160,192},{192,224},{224... | collective-permute-start | bytes 6152 | tf_op jit(solution)/shard_map/ppermute | solution.py:22
  355.4 12.2 %collective-permute-start.33 = (f32[24,1,8]{2,1,0:T(1,128)S(1)}, f32[24,1,8]{2,1,0:T(1,128)S(1)}, u32[]{:S(2)}, u32[]{:S(2)}) collective-permute-start(f32[24,1,8]{2,1,0:T(1,128)S(1)} %get-tuple-element.70), channel_id=1, source_target_pairs={{32,0},{64,32},{96,64},{128,96},{160,128},{192,160},{224,192},{256... | collective-permute-start | bytes 2312 | tf_op jit(solution)/shard_map/ppermute | solution.py:23
  357.4 13.7 %collective-permute-start.32 = (f32[24,1,8]{2,1,0:T(1,128)S(1)}, f32[24,1,8]{2,1,0:T(1,128)S(1)}, u32[]{:S(2)}, u32[]{:S(2)}) collective-permute-start(f32[24,1,8]{2,1,0:T(1,128)S(1)} %get-tuple-element.69), channel_id=1, source_target_pairs={{0,32},{32,64},{64,96},{96,128},{128,160},{160,192},{192,224},{224... | collective-permute-start | bytes 2312 | tf_op jit(solution)/shard_map/ppermute | solution.py:22
  362.7 12.1 %collective-permute-start.39 = (f32[32,12,2]{0,2,1:T(2,128)S(1)}, f32[32,12,2]{0,2,1:T(2,128)S(1)}, u32[]{:S(2)}, u32[]{:S(2)}) collective-permute-start(f32[32,12,2]{0,2,1:T(2,128)S(1)} %get-tuple-element.96), channel_id=1, source_target_pairs={{1,0},{2,1},{3,2},{4,3},{5,4},{6,5},{7,6},{8,7},{9,8},{10,9},{11,1... | collective-permute-start | bytes 9224 | tf_op jit(solution)/shard_map/ppermute | solution.py:23
  367.7 207.3 %collective-permute-start.16 = (f32[24,1,32]{2,1,0:T(1,128)}, f32[24,1,32]{2,1,0:T(1,128)}, u32[]{:S(2)}, u32[]{:S(2)}) collective-permute-start(f32[24,1,32]{2,1,0:T(1,128)} %get-tuple-element.37), channel_id=1, source_target_pairs={{0,32},{32,64},{64,96},{96,128},{128,160},{160,192},{192,224},{224... | collective-permute-start | bytes 9224 | tf_op jit(solution)/shard_map/ppermute | solution.py:22
  371.0 167.3 %collective-permute-start.25 = (f32[24,1,16]{2,1,0:T(1,128)}, f32[24,1,16]{2,1,0:T(1,128)}, u32[]{:S(2)}, u32[]{:S(2)}) collective-permute-start(f32[24,1,16]{2,1,0:T(1,128)} %get-tuple-element.60), channel_id=1, source_target_pairs={{32,0},{64,32},{96,64},{128,96},{160,128},{192,160},{224,192},{256... | collective-permute-start | bytes 4616 | tf_op jit(solution)/shard_map/ppermute | solution.py:23
  389.5 90.8 %collective-permute-start.41 = (f32[24,1,4]{0,2,1:T(4,128)}, f32[24,1,4]{0,2,1:T(4,128)}, u32[]{:S(2)}, u32[]{:S(2)}) collective-permute-start(f32[24,1,4]{0,2,1:T(4,128)} %get-tuple-element.138), channel_id=1, source_target_pairs={{32,0},{64,32},{96,64},{128,96},{160,128},{192,160},{224,192},{256... | collective-permute-start | bytes 1160 | tf_op jit(solution)/shard_map/ppermute | solution.py:23
  394.1 91.2 %collective-permute-start.40 = (f32[24,1,4]{0,2,1:T(4,128)}, f32[24,1,4]{0,2,1:T(4,128)}, u32[]{:S(2)}, u32[]{:S(2)}) collective-permute-start(f32[24,1,4]{0,2,1:T(4,128)} %get-tuple-element.137), channel_id=1, source_target_pairs={{0,32},{32,64},{64,96},{96,128},{128,160},{160,192},{192,224},{224... | collective-permute-start | bytes 1160 | tf_op jit(solution)/shard_map/ppermute | solution.py:22
  529.2 12.7 %collective-permute-start.24 = (f32[24,1,16]{2,1,0:T(1,128)S(1)}, f32[24,1,16]{2,1,0:T(1,128)S(1)}, u32[]{:S(2)}, u32[]{:S(2)}) collective-permute-start(f32[24,1,16]{2,1,0:T(1,128)S(1)} %copy-done.15), channel_id=1, source_target_pairs={{0,32},{32,64},{64,96},{96,128},{128,160},{160,192},{192,224},{224... | collective-permute-start | bytes 4616 | tf_op jit(solution)/shard_map/ppermute | solution.py:22
  543.9 11.7 %collective-permute-start.59 = (f32[3,18,1]{2,1,0:T(8,128)S(1)}, f32[3,18,1]{2,1,0:T(8,128)S(1)}, u32[]{:S(2)}, u32[]{:S(2)}) collective-permute-start(f32[3,18,1]{2,1,0:T(8,128)S(1)} %get-tuple-element.102), channel_id=1, source_target_pairs={{1,0},{2,1},{3,2},{4,3},{5,4},{6,5},{7,6},{8,7},{9,8},{10,9},{11,1... | collective-permute-start | bytes 656 | tf_op jit(solution)/shard_map/ppermute | solution.py:23
  576.4 12.5 %collective-permute-start.63 = (f32[3,34,1]{2,1,0:T(8,128)S(1)}, f32[3,34,1]{2,1,0:T(8,128)S(1)}, u32[]{:S(2)}, u32[]{:S(2)}) collective-permute-start(f32[3,34,1]{2,1,0:T(8,128)S(1)} %get-tuple-element.86), channel_id=1, source_target_pairs={{1,0},{2,1},{3,2},{4,3},{5,4},{6,5},{7,6},{8,7},{9,8},{10,9},{11,1... | collective-permute-start | bytes 1232 | tf_op jit(solution)/shard_map/ppermute | solution.py:23
  578.3 10.6 %collective-permute-start.62 = (f32[3,34,1]{2,1,0:T(8,128)S(1)}, f32[3,34,1]{2,1,0:T(8,128)S(1)}, u32[]{:S(2)}, u32[]{:S(2)}) collective-permute-start(f32[3,34,1]{2,1,0:T(8,128)S(1)} %get-tuple-element.85), channel_id=1, source_target_pairs={{0,1},{1,2},{2,3},{3,4},{4,5},{5,6},{6,7},{7,8},{8,9},{9,10},{10,1... | collective-permute-start | bytes 1232 | tf_op jit(solution)/shard_map/ppermute | solution.py:22
  581.6 11.9 %collective-permute-start.19 = (f32[24,34,1]{2,1,0:T(8,128)}, f32[24,34,1]{2,1,0:T(8,128)S(1)}, u32[]{:S(2)}, u32[]{:S(2)}) collective-permute-start(f32[24,34,1]{2,1,0:T(8,128)} %get-tuple-element.42), channel_id=1, source_target_pairs={{1,0},{2,1},{3,2},{4,3},{5,4},{6,5},{7,6},{8,7},{9,8},{10,9},{11,1... | collective-permute-start | bytes 9800 | tf_op jit(solution)/shard_map/ppermute | solution.py:23
  586.9 12.3 %collective-permute-start.18 = (f32[24,34,1]{2,1,0:T(8,128)S(1)}, f32[24,34,1]{2,1,0:T(8,128)S(1)}, u32[]{:S(2)}, u32[]{:S(2)}) collective-permute-start(f32[24,34,1]{2,1,0:T(8,128)S(1)} %get-tuple-element.41), channel_id=1, source_target_pairs={{0,1},{1,2},{2,3},{3,4},{4,5},{5,6},{6,7},{7,8},{8,9},{9,10},{10,1... | collective-permute-start | bytes 9800 | tf_op jit(solution)/shard_map/ppermute | solution.py:22
  (62 other events, 549.0 us)
where the time goes:
time: 637 us; the launch traced here: 625 us
  local copies, waits for them, and re-layouts  252 us (40%)
  starting transfers between devices  214 us (34%)
  waiting for transfers between devices  56.2 us (9%)
  blocking collectives  54.1 us (8%)
  other arithmetic  45.2 us (7%)
    slice x70, local copies, waits for them, and re-layouts, shrink_axis(): lax.slice_in_dim(padded_in, begin, begin + 2 * out_len - 1, 2, along_axis)  205 us
    ppermute x34, starting transfers between devices, padded(): before = lax.ppermute(last, axis, up)  116 us
    ppermute x34, starting transfers between devices, padded(): after = lax.ppermute(first, axis, down)  97.4 us
    ppermute x34, waiting for transfers between devices, padded(): before = lax.ppermute(last, axis, up)  48.2 us
    all_gather x1, blocking collectives, local(): gathered = lax.all_gather(gathered, 'row', axis=1, tiled=True)  31.5 us
    all_gather x1, blocking collectives, local(): gathered = lax.all_gather(planes_all, 'col', axis=2, tiled=True)  22.7 us
    concatenate x30, other arithmetic, padded(): array = jnp.concatenate([before, array, after], axis=dim)  13.7 us
  transfers between devices with their start and end apart: 68, of which 20 were waited for; matrix products, arithmetic and copies ran while one was open for 22% of the time, Pallas kernels for 0%

commit v1 on v0

v1 whole, which is shorter than its diff:
```python
import numpy as np
import jax
import jax.numpy as jnp
import ml_dtypes
from jax import lax
from jax.experimental import pallas as pl
from jax.experimental.pallas import tpu as pltpu
from jax.sharding import PartitionSpec as P

V = 8
C = 3
BLOCK = 128
LANES = 128
F32 = jnp.float32
MESH = pl.DeviceIdType.MESH

SIDE = [BLOCK >> level for level in range(8)]
ROW0 = {1: 0, 2: 80, 3: 128, 4: 160}
ROWS = {1: 80, 2: 48, 3: 32, 4: 24}
LANE0 = {1: 0, 2: 80, 3: 0, 4: 32}
HALF = {1: 0, 2: 0, 3: 1, 4: 1}
ROW5, LANE5 = 184, 64
FLAT0 = {5: 0, 6: 49, 7: 74}
FLATW = {5: 7, 6: 5, 7: 4}
COPY0 = 73


def shrink_matrix(n):
    m = np.zeros((n // 2, n))
    for k in range(n // 2):
        for a, w in zip(range(-2, 3), (1.0, 4.0, 6.0, 4.0, 1.0)):
            if 0 <= 2 * k + a < n:
                m[k, 2 * k + a] += w / 16.0
    return m


def spread_matrix(n):
    m = np.zeros((2 * n, n))
    for k in range(n):
        for j, w in ((k - 1, 1 / 8), (k, 6 / 8), (k + 1, 1 / 8)):
            if 0 <= j < n:
                m[2 * k, j] += w
        for j in (k, k + 1):
            if j < n:
                m[2 * k + 1, j] += 0.5
    return m


def tile_constants():
    tiles = 10
    total = tiles * BLOCK
    down = [np.eye(total)]
    for level in range(7):
        down.append(shrink_matrix(total >> level) @ down[-1])
    step = [spread_matrix(total >> (level + 1)) for level in range(7)]
    up = [None, step[0]]
    for level in range(1, 7):
        up.append(up[-1] @ step[level])

    def rows_of(matrix, level, t, low, high):
        n = SIDE[level]
        out = np.zeros((high - low + 1, matrix.shape[1]))
        for i, k in enumerate(range(n * t + low, n * t + high + 1)):
            if 0 <= k < matrix.shape[0]:
                out[i] = matrix[k]
        return out

    mats, cols, rows = [], [], []
    for t in (0, 1, 5, 8, 9):
        here = slice(BLOCK * t, BLOCK * (t + 1))
        wide = {l: rows_of(down[l], l, t, -4, SIDE[l] + 4) for l in range(1, 5)}
        parts = []
        for l in range(1, 5):
            span = slice(LANE0[l], LANE0[l] + SIDE[l] + 9)
            own, finer = np.zeros((BLOCK, LANES)), np.zeros((BLOCK, LANES))
            own[:, span] = wide[l][:, here].T
            finer[:, span] = -rows_of(step[l] @ down[l + 1], l, t, -4, SIDE[l] + 4)[:, here].T
            parts += [own, finer]
        copies = np.zeros((BLOCK, LANES))
        one = wide[1][:, here].T
        copies[:, 3:69] = one[:, 3:69]
        copies[:, COPY0 : COPY0 + 2] = one[:, 3:5]
        copies[:, COPY0 + 2 : COPY0 + 4] = one[:, 67:69]
        parts.append(copies)
        column_sum, row_sum = np.zeros((1, LANES)), np.zeros((1, LANES))
        for l in (5, 6, 7):
            w, f = FLATW[l], FLAT0[l]
            local = rows_of(down[l], l, t, -1, w - 2)[:, here]
            flat = np.zeros((BLOCK, LANES))
            flat[:, f : f + w] = local.T
            parts.append(flat)
            total_of = local.sum(axis=1)
            column_sum[0, f : f + w * w] = np.tile(total_of, w)
            row_sum[0, f : f + w * w] = np.repeat(total_of, w)
        mats.append(np.concatenate(parts))

        expand_a, expand_b = np.zeros((LANES, BLOCK)), np.zeros((LANES, BLOCK))
        row_a, row_b = np.zeros((BLOCK, LANES)), np.zeros((BLOCK, LANES))
        for l in range(1, 6):
            n = SIDE[l]
            for k in range(-1, n + 2):
                g = n * t + k
                if not 0 <= g < up[l].shape[1]:
                    continue
                weights = up[l][here, g]
                lane = LANE0[l] + k + 4 if l < 5 else LANE5 + k + 1
                row = ROW0[l] + k + 4 if l < 5 else ROW5 + k + 1
                if l < 3:
                    expand_a[lane] = weights
                    row_a[:, row] = weights
                else:
                    expand_b[lane] = weights
                    row_b[:, row - 128] = weights
        spread_rows, spread_lanes = np.zeros((3, 184, LANES)), np.zeros((8, LANES))
        for d in range(3):
            block = slice(BLOCK * (t + d - 1), BLOCK * (t + d))
            if not 0 <= t + d - 1 < tiles:
                continue
            for l in range(1, 5):
                share = wide[l][:, block].sum(axis=1)
                spread_rows[d, ROW0[l] : ROW0[l] + SIDE[l] + 9] = share[:, None]
                spread_lanes[2 * d + HALF[l], LANE0[l] : LANE0[l] + SIDE[l] + 9] = share
        spread_lanes[6] = column_sum
        weight_of = down[7][:, here].sum(axis=0)
        spread_lanes[7] = weight_of
        cols.append(np.concatenate([expand_a, expand_b, spread_lanes]))
        rows.append(
            np.concatenate(
                [row_a, row_b, spread_rows.reshape(-1, LANES), np.repeat(weight_of[:, None], LANES, 1), np.repeat(row_sum, 8, 0)]
            )
        )
    mats = np.stack(mats).astype(np.float32)
    high = mats.astype(ml_dtypes.bfloat16)
    low = (mats - high.astype(np.float32)).astype(ml_dtypes.bfloat16)
    split = np.stack([high, low], axis=1)

    flat = np.zeros((2, LANES, LANES))
    for which, l in ((0, 7), (1, 6)):
        w, v = FLATW[l], FLATW[l - 1]
        local = np.zeros((v, w))
        for i in range(v):
            m, odd = divmod(i - 1, 2)
            for j, weight in ((m, 0.5), (m + 1, 0.5)) if odd else ((m - 1, 1 / 8), (m, 6 / 8), (m + 1, 1 / 8)):
                local[i, j + 1] += weight
        kron = np.einsum("ai,bj->ijab", local, local).reshape(w * w, v * v)
        flat[which, FLAT0[l] : FLAT0[l] + w * w, FLAT0[l - 1] : FLAT0[l - 1] + v * v] = kron
    return split, np.stack(cols).astype(np.float32), np.stack(rows).astype(np.float32), flat.astype(np.float32)


MATS, COLS, ROWC, FLAT = tile_constants()
N_MATS, N_COLS, N_ROWC = MATS.shape[2], COLS.shape[1], ROWC.shape[1]
COPY_AT = 1024
FLAT_AT = {5: 1152, 6: 1280, 7: 1408}
SPREAD_AT, WEIGHT_AT, RSUM_AT = 256, 808, 936

BEYOND = (1, -1, 2, -2, 3, -3)
AROUND = [(a, b) for a in (-1, 0, 1) for b in (-1, 0, 1) if a or b]
ITEMS = [(c, l, ROW0[l] + 8 * i) for c in range(C) for l in range(1, 5) for i in range(ROWS[l] // 8)]
ITEMS = [item for item in ITEMS if item[2] - ROW0[item[1]] < SIDE[item[1]] + 9]
SIDE_TILES = -(-len(ITEMS) // 16)


def split_dot(a, mat_ref, at, depth, exact=False):
    high = a.astype(jnp.bfloat16)
    low = (a - high.astype(F32)).astype(jnp.bfloat16)
    m_high = mat_ref[0, at : at + depth, :]
    out = jnp.dot(high, m_high, preferred_element_type=F32) + jnp.dot(low, m_high, preferred_element_type=F32)
    if not exact:
        out = out + jnp.dot(high, mat_ref[1, at : at + depth, :], preferred_element_type=F32)
    return out


def lanes_in(low, high, shape=(1, LANES)):
    lane = lax.broadcasted_iota(jnp.int32, shape, len(shape) - 1)
    return jnp.logical_and(lane >= low, lane < high)


def keep(value, low, high):
    return jnp.where(lanes_in(low, high), value, 0.0)


def turn(value, shift):
    shift = shift % LANES
    return pltpu.roll(value, shift, value.ndim - 1) if shift else value


def make_kernel(nr, nc):
    cells = float(nr * nc)

    def kernel(bits_ref, label_ref, x_hbm, mats_hbm, cols_hbm, rows_hbm, flat_hbm, out_ref, *scratch):
        (x_ref, mats, cols, rowc, flat, s1, s2, s3, s4, s5, s6, s7, e1, e2, e3, e4, d1, d2, d3, d4, copies_ref, xs_ref,
         planes, ones_ref, m_send, m_col, m_row, mask_send, mask_recv, t_send, t_row, t_col, v_send, v_recv, h_send,
         h_recv, w_ref, load_sem, send_sem, recv_sem) = scratch
        s = {1: s1, 2: s2, 3: s3, 4: s4, 5: s5, 6: s6, 7: s7}
        e = {1: e1, 2: e2, 3: e3, 4: e4}
        d = {1: d1, 2: d2, 3: d3, 4: d4}
        r = lax.axis_index("row")
        c_at = lax.axis_index("col")

        def place(t, n):
            return jnp.where(t == 0, 0, jnp.where(t == 1, 1, jnp.where(t == n - 1, 4, jnp.where(t == n - 2, 3, 2))))

        def device(dr, dc):
            return (lax.rem(r + dr + nr, nr), lax.rem(c_at + dc + nc, nc))

        def inside(dr, dc):
            rr, cc = r + dr, c_at + dc
            ok = jnp.logical_and(jnp.logical_and(rr >= 0, rr < nr), jnp.logical_and(cc >= 0, cc < nc))
            return ok.astype(jnp.int32).astype(F32)

        row_place, col_place = place(r, nr), place(c_at, nc)
        loads = [
            pltpu.make_async_copy(x_hbm, x_ref, load_sem.at[0]),
            pltpu.make_async_copy(rows_hbm.at[row_place], rowc, load_sem.at[1]),
            pltpu.make_async_copy(cols_hbm.at[col_place], cols, load_sem.at[2]),
            pltpu.make_async_copy(mats_hbm.at[col_place], mats, load_sem.at[3]),
            pltpu.make_async_copy(flat_hbm, flat, load_sem.at[4]),
        ]
        for load in loads:
            load.start()

        barrier = pltpu.get_barrier_semaphore()
        partners = [(0, i) for i in range(1, nc)] + [(i, 0) for i in range(1, nr)]
        partners += [(a, b) for a, b in AROUND if a and b]
        for a, b in partners:
            pl.semaphore_signal(barrier, inc=1, device_id=device(a, b), device_id_type=MESH)

        used = [0]
        sent = []

        def post(src, dst, to):
            slot = used[0]
            used[0] += 1
            copy = pltpu.make_async_remote_copy(
                src_ref=src, dst_ref=dst, send_sem=send_sem.at[slot], recv_sem=recv_sem.at[slot],
                device_id=device(*to), device_id_type=MESH,
            )
            copy.start()
            sent.append(copy)
            return copy

        view = lax.broadcasted_iota(jnp.int32, (V, LANES), 0)
        lane = lax.broadcasted_iota(jnp.int32, (V, LANES), 1)
        bits = jnp.full((V, LANES), bits_ref[0, 0], jnp.int32)
        label = jnp.full((V, LANES), label_ref[0, 0], jnp.int32)
        own_mask = jnp.bitwise_and(jnp.right_shift(bits, view), 1).astype(F32)
        own_mask = own_mask * jnp.where(label == view, 4.0, 1.0)
        mask_send[...] = own_mask

        for l in range(1, 8):
            n = SIDE[l]
            s[l][0:3] = jnp.zeros((3, 24, LANES), F32)
            s[l][n + 6 :] = jnp.zeros((s[l].shape[0] - n - 6, 24, LANES), F32)
        for l in range(1, 5):
            e[l][SIDE[l] + 9 :] = jnp.zeros((ROWS[l] - SIDE[l] - 9, 24, LANES), F32)
        w_ref[...] = jnp.zeros_like(w_ref)

        loads[0].wait()
        loads[1].wait()
        loads[2].wait()

        weight_rows = rowc[WEIGHT_AT : WEIGHT_AT + BLOCK, :]
        weight_cols = cols[256 + 7 : 256 + 8, :]
        mean = jnp.zeros((1, LANES), F32)
        for c in range(C):
            parts = []
            for v in range(V):
                weighted = x_ref[(v * C + c) * BLOCK : (v * C + c + 1) * BLOCK, :] * weight_rows
                parts.append(jnp.sum(weighted.reshape(16, 8, LANES), axis=0)[None])
            both = jnp.sum(jnp.concatenate(parts, axis=0), axis=1) * weight_cols
            total = jnp.sum(both, axis=1, keepdims=True)
            mean = mean + jnp.sum(jnp.where(lane == view + V * c, total, 0.0), axis=0, keepdims=True)
        m_send[0] = mean * (1.0 / cells)

        pl.semaphore_wait(barrier, len(partners))
        m_cols = [post(m_send.at[0], m_col.at[i - 1], (0, i)) for i in range(1, nc)]
        masks = [post(mask_send, mask_recv.at[i], to) for i, to in enumerate(AROUND)]

        def pixel_row(row):
            return jnp.concatenate(
                [x_ref[pl.ds(c * BLOCK + row, V, stride=C * BLOCK), :] for c in range(C)], axis=0
            )

        def tap(get, k):
            total = None
            for a, w in zip(range(-2, 3), (1.0, 4.0, 6.0, 4.0, 1.0)):
                term = get(2 * k + a)
                if term is not None:
                    term = term * (w / 16.0)
                    total = term if total is None else total + term
            return total

        def edge_row(row):
            return pixel_row(row) if 0 <= row < BLOCK else None

        for k in (-1, 0, 63, 64):
            s1[k + 4] = tap(edge_row, k)

        def first_pair(i, carry):
            rows = [pixel_row(4 * i + j) for j in range(7)]
            for half in range(2):
                total = None
                for j, w in enumerate((1.0, 4.0, 6.0, 4.0, 1.0)):
                    term = rows[2 * half + j] * (w / 16.0)
                    total = term if total is None else total + term
                s1[2 * i + half + 5] = total
            return carry

        lax.fori_loop(0, 31, first_pair, 0)
        s1[69] = jnp.zeros((24, LANES), F32)
        not_first = jnp.where(r > 0, 1.0, 0.0)
        not_last = jnp.where(r < nr - 1, 1.0, 0.0)
        not_near = jnp.where(r < nr - 2, 1.0, 0.0)

        def trim(l):
            n = SIDE[l]
            s[l][3] = s[l][3] * not_first
            s[l][n + 4] = s[l][n + 4] * not_last
            s[l][n + 5] = s[l][n + 5] * (not_last if l < 7 else not_near)

        trim(1)
        for l in range(2, 8):
            n = SIDE[l]
            src, dst = s[l - 1], s[l]

            def one(i, src=src, dst=dst):
                total = None
                for j, w in enumerate((1.0, 4.0, 6.0, 4.0, 1.0)):
                    term = src[2 * i + j] * (w / 16.0)
                    total = term if total is None else total + term
                dst[i + 3] = total

            if l == 2:
                def five(i, carry, one=one):
                    for j in range(5):
                        one(5 * i + j)
                    return carry

                lax.fori_loop(0, 7, five, 0)
            else:
                for i in range(n + 3):
                    one(i)
            trim(l)

        loads[3].wait()
        loads[4].wait()
        tops = jnp.zeros((24, LANES), F32)
        for l in (5, 6, 7):
            w = FLATW[l]
            flat_l = split_dot(s[l][3 : 3 + w].reshape(w * 24, LANES), mats, FLAT_AT[l], BLOCK).reshape(w, 24, LANES)
            for i in range(w):
                tops = tops + turn(flat_l[i], i * w)
        t_send[0, 0:24] = tops
        t_send[0, 24:32] = own_mask * (rowc[RSUM_AT : RSUM_AT + 1, :] * cols[256 + 6 : 256 + 7, :])
        t_rows = [post(t_send.at[0], t_row.at[i], (off, 0)) for i, off in enumerate(BEYOND)]

        for l in range(1, 5):
            n, src, dst = SIDE[l], s[l + 1], e[l]

            def pair(i, src=src, dst=dst):
                x0, x1, x2 = src[i + 1], src[i + 2], src[i + 3]
                dst[2 * i] = (x0 + x2) * 0.125 + x1 * 0.75
                return (x1 + x2) * 0.5

            half = n // 2 + 4
            if l < 3:
                def pairs(i, carry, pair=pair, dst=dst):
                    for j in range(4):
                        dst[2 * (4 * i + j) + 1] = pair(4 * i + j)
                    return carry

                lax.fori_loop(0, half // 4, pairs, 0)
            else:
                for i in range(half):
                    dst[2 * i + 1] = pair(i)
            dst[n + 8] = (src[half + 1] + src[half + 3]) * 0.125 + src[half + 2] * 0.75

        chunk = {1: 16, 2: 16, 3: 16, 4: 24}
        for l in range(1, 5):
            m = chunk[l]

            def details(i, carry, l=l, m=m):
                at = pl.multiple_of(i * m, m)
                both = jnp.concatenate(
                    [s[l][pl.ds(at, m)].reshape(m * 24, LANES), e[l][pl.ds(at, m)].reshape(m * 24, LANES)], axis=1
                )
                d[l][pl.ds(at, m)] = split_dot(both, mats, 256 * (l - 1), 256).reshape(m, 24, LANES)
                if l == 1:
                    only = split_dot(both[:, :LANES], mats, COPY_AT, BLOCK, exact=True)
                    copies_ref[pl.ds(at, m)] = only.reshape(m, 24, LANES)
                return carry

            lax.fori_loop(0, ROWS[l] // m, details, 0)

        for copy in m_cols:
            copy.wait_recv()
        m_send[1] = m_send[0] + jnp.sum(m_col[...], axis=0)
        m_rows = [post(m_send.at[1], m_row.at[i - 1], (i, 0)) for i in range(1, nr)]

        def weights(mask):
            total = jnp.sum(mask, axis=0, keepdims=True)
            return mask / jnp.where(total > 0.0, total, 1.0)

        own_weights = weights(own_mask)
        for c in range(C):
            total = None
            for v in range(V):
                term = x_ref[(v * C + c) * BLOCK : (v * C + c + 1) * BLOCK, :] * own_weights[v : v + 1, :]
                total = term if total is None else total + term
            xs_ref[c] = total

        def gather_tops(own, recv, stride, at):
            total = own
            for i, off in enumerate(BEYOND):
                got = recv[i]
                step = -off
                moved = None
                for l in (5, 6, 7):
                    w, n, f = FLATW[l], SIDE[l], FLAT0[l]
                    if w <= n * abs(step):
                        continue
                    index = lax.broadcasted_iota(jnp.int32, (1, LANES), 1) - f
                    along = index // w if stride == "row" else index % w
                    ok = lanes_in(f, f + w * w)
                    ok = jnp.logical_and(ok, jnp.logical_and(along - n * step >= 0, along - n * step < w))
                    term = jnp.where(ok, turn(got, n * step * (w if stride == "row" else 1)), 0.0)
                    moved = term if moved is None else moved + term
                total = total + moved * (inside(step, 0) if stride == "row" else inside(0, step))
            return total

        for copy in t_rows:
            copy.wait_recv()
        t_send[1] = gather_tops(t_send[0], t_row, "row", r)
        t_cols = [post(t_send.at[1], t_col.at[i], (0, off)) for i, off in enumerate(BEYOND)]

        for copy in masks:
            copy.wait_recv()
        around = {(0, 0): own_mask}
        for i, (a, b) in enumerate(AROUND):
            around[(-a, -b)] = mask_recv[i] * inside(-a, -b)
        inner = [
            [
                sum(around[(a, b)] * cols[256 + 2 * (b + 1) + h : 257 + 2 * (b + 1) + h, :] for b in (-1, 0, 1))
                for a in (-1, 0, 1)
            ]
            for h in range(2)
        ]

        def side_weights(a):
            left, mid, right = (weights(around[(a, b)]) for b in (-1, 0, 1))
            value = jnp.where(jnp.logical_and(lane >= COPY0, lane < COPY0 + 2), left, mid)
            return jnp.where(jnp.logical_and(lane >= COPY0 + 2, lane < COPY0 + 4), right, value)

        row_weights = {a: side_weights(a) for a in (-1, 0, 1)}

        for l in range(1, 5):

            def blend(i, carry, l=l):
                at = pl.multiple_of(i * 8, 8)
                row = pl.multiple_of(ROW0[l] + i * 8, 8)
                mask = None
                for a in range(3):
                    term = rowc[pl.ds(SPREAD_AT + 184 * a + row, 8), :][:, None, :] * inner[HALF[l]][a][None]
                    mask = term if mask is None else mask + term
                whole = jnp.sum(mask, axis=1)
                inverse = jnp.where(whole > 0.0, 1.0 / jnp.where(whole > 0.0, whole, 1.0), 0.0)
                for c in range(C):
                    part = d[l][pl.ds(at, 8), V * c : V * c + V, :]
                    planes[c, pl.ds(row, 8), :] = jnp.sum(part * mask, axis=1) * inverse
                    if l == 1:
                        part = copies_ref[pl.ds(at, 8), V * c : V * c + V, :]
                        ones_ref[c, pl.ds(at, 8), :] = jnp.sum(part * row_weights[0][None], axis=1)
                return carry

            lax.fori_loop(0, ROWS[l] // 8, blend, 0)

        for c in range(C):
            v_send[0, c, 0] = planes[c, 0:8] + planes[c, 80:88]
            v_send[0, c, 1] = planes[c, 128:136] + planes[c, 160:168]
            part = copies_ref[0:8, V * c : V * c + V, :]
            v_send[0, c, 2] = jnp.sum(part * row_weights[-1][None], axis=1)
            v_send[1, c, 0] = planes[c, 67:75] + planes[c, 115:123]
            v_send[1, c, 1] = planes[c, 147:155] + planes[c, 171:179]
            part = copies_ref[67:75, V * c : V * c + V, :]
            v_send[1, c, 2] = jnp.sum(part * row_weights[1][None], axis=1)
        v_rows = [post(v_send.at[0], v_recv.at[0], (-1, 0)), post(v_send.at[1], v_recv.at[1], (1, 0))]

        for copy in t_cols:
            copy.wait_recv()
        tops_all = gather_tops(t_send[1], t_col, "col", c_at)
        images, mask = tops_all[0:24], tops_all[24:32]
        whole = jnp.sum(mask, axis=0, keepdims=True)
        here = whole > 0.0
        share = mask * jnp.where(here, 1.0 / jnp.where(here, whole, 1.0), 0.0)
        finer = jnp.dot(images, flat[0] + flat[1], precision=lax.Precision.HIGHEST, preferred_element_type=F32)
        detail = images - finer
        blended = [jnp.sum(detail[V * c : V * c + V] * share, axis=0, keepdims=True) for c in range(C)]
        balance = keep(jnp.sum(share, axis=0, keepdims=True) * (1.0 / V) - share, FLAT0[7], FLAT0[7] + 16)
        chain = jnp.concatenate(blended + [jnp.zeros((8 - C, LANES), F32), balance], axis=0)
        for which in range(2):
            step = jnp.dot(chain, flat[which], precision=lax.Precision.HIGHEST, preferred_element_type=F32)
            chain = chain + jnp.where(here, step, 0.0)
        for c in range(C):
            w_ref[V * c : V * c + V] = chain[8:16]

        for copy in v_rows:
            copy.wait_recv()
        for which, away in ((1, -1), (0, 1)):
            flag = inside(away, 0)
            for c in range(C):
                for l in range(1, 5):
                    at = ROW0[l] + (3 if away < 0 else SIDE[l])
                    low = LANE0[l]
                    got = v_recv[which, c, HALF[l]][0:6] * flag
                    planes[c, at : at + 6] += keep(got, low, low + SIDE[l] + 9)
                at = 3 if away < 0 else SIDE[1]
                ones_ref[c, at : at + 6] += v_recv[which, c, 2][0:6] * flag
        for which in range(2):
            for g in range(SIDE_TILES):
                tile = jnp.zeros((8, LANES), F32)
                for u, (c, l, row) in enumerate(ITEMS[16 * g : 16 * g + 16]):
                    first = LANE0[l] + (SIDE[l] + 3 if which else 0)
                    tile = tile + keep(turn(planes[c, row : row + 8], 8 * u - first), 8 * u, 8 * u + 6)
                    if l == 1:
                        slot, first = (8 * u, COPY0 + 2) if which else (8 * u + 3, COPY0)
                        tile = tile - keep(turn(ones_ref[c, row : row + 8], slot - first), slot, slot + 2)
                h_send[which, g] = tile
        h_cols = [post(h_send.at[0], h_recv.at[0], (0, -1)), post(h_send.at[1], h_recv.at[1], (0, 1))]

        for c in range(C):
            planes[c, 0:80] -= keep(ones_ref[c], 0, COPY0)
            planes[c, ROW5 : ROW5 + 8] = jnp.zeros((8, LANES), F32)

        for copy in m_rows:
            copy.wait_recv()
        means = m_send[1] + jnp.sum(m_row[...], axis=0)
        picked = jnp.where(lane // V == view, jnp.broadcast_to(means, (V, LANES)), 0.0)
        level5 = chain[0:8] + jnp.dot(picked, w_ref[...], precision=lax.Precision.HIGHEST, preferred_element_type=F32)
        for i in range(7):
            line = keep(turn(level5, LANE5 - 7 * i), LANE5, LANE5 + 7)
            for c in range(C):
                planes[c, ROW5 + i : ROW5 + i + 1] = line[c : c + 1]

        for copy in h_cols:
            copy.wait_recv()
        for which, away in ((1, -1), (0, 1)):
            flag = inside(0, away)
            for i, (c, l, row) in enumerate(ITEMS):
                u = i % 16
                first = LANE0[l] + (3 if away < 0 else SIDE[l])
                got = h_recv[which, i // 16] * flag
                planes[c, row : row + 8] += keep(turn(got, first - 8 * u), first, first + 6)

        for c in range(C):
            upper = jnp.dot(rowc[0:128], planes[c, 0:128], precision=lax.Precision.HIGH, preferred_element_type=F32)
            lower = jnp.dot(rowc[128:256, 0:64], planes[c, 128:192], precision=lax.Precision.HIGH, preferred_element_type=F32)
            total = jnp.dot(upper, cols[0:128], precision=lax.Precision.HIGH, preferred_element_type=F32)
            total = total + jnp.dot(lower, cols[128:256], precision=lax.Precision.HIGH, preferred_element_type=F32)
            out_ref[c] = xs_ref[c] + total

        for copy in sent:
            copy.wait_send()

    def vmem(*shape):
        return pltpu.VMEM(shape, F32)

    slabs = [vmem(n, 24, LANES) for n in (80, 48, 32, 24, 16, 16, 16)]
    wides = [vmem(ROWS[l], 24, LANES) for l in range(1, 5)]
    scratch = [
        vmem(V * C * BLOCK, LANES),
        pltpu.VMEM((2, N_MATS, LANES), jnp.bfloat16),
        vmem(N_COLS, LANES),
        vmem(N_ROWC, LANES),
        vmem(2, LANES, LANES),
        *slabs, *wides, *wides,
        vmem(80, 24, LANES),
        vmem(C, BLOCK, LANES),
        vmem(C, 192, LANES),
        vmem(C, 80, LANES),
        vmem(2, 1, LANES),
        vmem(nc - 1, 1, LANES),
        vmem(nr - 1, 1, LANES),
        vmem(V, LANES),
        vmem(8, V, LANES),
        vmem(2, 32, LANES),
        vmem(6, 32, LANES),
        vmem(6, 32, LANES),
        vmem(2, C, 3, 8, LANES),
        vmem(2, C, 3, 8, LANES),
        vmem(2, SIDE_TILES, 8, LANES),
        vmem(2, SIDE_TILES, 8, LANES),
        vmem(LANES, LANES),
        pltpu.SemaphoreType.DMA((5,)),
        pltpu.SemaphoreType.DMA((nr + nc + 22,)),
        pltpu.SemaphoreType.DMA((nr + nc + 22,)),
    ]
    return pl.pallas_call(
        kernel,
        out_shape=jax.ShapeDtypeStruct((C, BLOCK, BLOCK), F32),
        in_specs=[pl.BlockSpec(memory_space=pltpu.SMEM)] * 2 + [pl.BlockSpec(memory_space=pl.ANY)] * 5,
        out_specs=pl.BlockSpec(memory_space=pltpu.VMEM),
        scratch_shapes=scratch,
        compiler_params=pltpu.CompilerParams(collective_id=0, has_side_effects=True, vmem_limit_bytes=48 << 20),
    )


def solution(mesh):
    call = make_kernel(mesh.shape["row"], mesh.shape["col"])

    def local(view_images, intersection_bits, seam_labels):
        planes = view_images.reshape(V * C * BLOCK, BLOCK)
        return call(
            intersection_bits, seam_labels, planes,
            jnp.asarray(MATS), jnp.asarray(COLS), jnp.asarray(ROWC), jnp.asarray(FLAT),
        )

    placed = (P(None, None, "row", "col"), P("row", "col"), P("row", "col"))
    return jax.shard_map(local, mesh=mesh, in_specs=placed, out_specs=P(None, "row", "col"), check_vma=False)
```

time: 637 us -> 43 us (0.07)
  the two profiles are of different devices: /device:TPU:112 before, /device:TPU:1 now
where the time goes in v1:
time: 43 us; the launch traced here: 42.7 us
  Pallas kernels  35.6 us (83%)
  local copies, waits for them, and re-layouts  5.76 us (13%)
  between operations  1.32 us (3%)
    pallas_call x1, Pallas kernels, local(): call(intersection_bits, seam_labels, planes, jnp.asarray(MATS), jnp.asarr...  35.6 us
    unnamed x9, local copies, waits for them, and re-layouts  5.76 us

profile of v1, /device:TPU:1, one launch (start us, length us, event | category | flops | bytes accessed | tf_op | source)
XLA Modules:
  0.0 42.7 jit_solution(18019160823415131524)
XLA Ops:
  1.3 0.0 copy-start
  1.3 1.7 %copy-done = f32[5,944,128]{2,1,0:T(8,128)S(1)} copy-done((f32[5,944,128]{2,1,0:T(8,128)S(1)}, f32[5,944,128]{2,1,0:T(8,128)}, u32[]{:S(2)}) %copy-start) | copy-done | bytes 2416664
  3.0 0.0 copy-start.1
  3.0 1.4 %copy-done.1 = f32[8,3,128,128]{3,2,1,0:T(8,128)S(1)} copy-done((f32[8,3,128,128]{3,2,1,0:T(8,128)S(1)}, f32[8,3,128,128]{3,2,1,0:T(8,128)}, u32[]{:S(2)}) %copy-start.1) | copy-done | bytes 1572888
  4.4 0.0 copy-start.2
  4.4 1.1 %copy-done.2 = f32[5,264,128]{2,1,0:T(8,128)S(1)} copy-done((f32[5,264,128]{2,1,0:T(8,128)S(1)}, f32[5,264,128]{2,1,0:T(8,128)}, u32[]{:S(2)}) %copy-start.2) | copy-done | bytes 675864
  5.5 0.0 copy-start.3
  5.5 0.9 %copy-done.3 = f32[2,128,128]{2,1,0:T(8,128)S(1)} copy-done((f32[2,128,128]{2,1,0:T(8,128)S(1)}, f32[2,128,128]{2,1,0:T(8,128)}, u32[]{:S(2)}) %copy-start.3) | copy-done | bytes 131096
  6.4 35.6 %shard_map.73 = f32[3,128,128]{2,1,0:T(8,128)S(1)} custom-call(s32[1,1]{1,0:T(1,128)S(6)} %copy.9.bits_ref, s32[1,1]{1,0:T(1,128)S(6)} %copy.10.label_ref, f32[3072,128]{1,0:T(8,128)S(1)} %bitcast.1, bf16[5,2,1536,128]{3,2,1,0:T(8,128)(2,1)} %constant.8.clone.mats_hbm, f32[5,264,128]{2,1,0:T(8,128)S(1)} %copy-done.2, f32[5,944,128]{2,1,0:T(8,128)S(1)} %copy-done, ...), custom_call_target="tpu_custom_call" | custom-call | tf_op jit(solution)/shard_map/pallas_call | solution.py:612
  42.0 0.7 %copy.11 = f32[3,128,128]{2,1,0:T(8,128)} copy(f32[3,128,128]{2,1,0:T(8,128)S(1)} %shard_map.73) | data formatting | bytes 393216
Async XLA Ops:
  1.3 1.7 %copy-start = (f32[5,944,128]{2,1,0:T(8,128)S(1)}, f32[5,944,128]{2,1,0:T(8,128)}, u32[]{:S(2)}) copy-start(f32[5,944,128]{2,1,0:T(8,128)} %constant.10.clone.rows_hbm) | copy-start | bytes 7249924
  3.0 1.4 %copy-start.1 = (f32[8,3,128,128]{3,2,1,0:T(8,128)S(1)}, f32[8,3,128,128]{3,2,1,0:T(8,128)}, u32[]{:S(2)}) copy-start(f32[8,3,128,128]{3,2,1,0:T(8,128)} %param.7) | copy-start | bytes 4718596
  4.4 1.1 %copy-start.2 = (f32[5,264,128]{2,1,0:T(8,128)S(1)}, f32[5,264,128]{2,1,0:T(8,128)}, u32[]{:S(2)}) copy-start(f32[5,264,128]{2,1,0:T(8,128)} %constant.9.clone.cols_hbm) | copy-start | bytes 2027524
  5.5 0.9 %copy-start.3 = (f32[2,128,128]{2,1,0:T(8,128)S(1)}, f32[2,128,128]{2,1,0:T(8,128)}, u32[]{:S(2)}) copy-start(f32[2,128,128]{2,1,0:T(8,128)} %constant.11.clone.flat_hbm) | copy-start | bytes 393220

commit v2 on v1

--- a/solution.py
+++ b/solution.py
@@ -69,30 +69,34 @@
     for t in (0, 1, 5, 8, 9):
         here = slice(BLOCK * t, BLOCK * (t + 1))
         wide = {l: rows_of(down[l], l, t, -4, SIDE[l] + 4) for l in range(1, 5)}
-        parts = []
+        parts = {}
         for l in range(1, 5):
             span = slice(LANE0[l], LANE0[l] + SIDE[l] + 9)
             own, finer = np.zeros((BLOCK, LANES)), np.zeros((BLOCK, LANES))
-            own[:, span] = wide[l][:, here].T
-            finer[:, span] = -rows_of(step[l] @ down[l + 1], l, t, -4, SIDE[l] + 4)[:, here].T
-            parts += [own, finer]
+            own[:, span] = wide[l][:, here].T / 16.0**l
+            finer[:, span] = -rows_of(step[l] @ down[l + 1], l, t, -4, SIDE[l] + 4)[:, here].T / (8 * 16.0 ** (l + 1))
+            parts[l] = np.concatenate([own, finer])
         copies = np.zeros((BLOCK, LANES))
-        one = wide[1][:, here].T
+        one = wide[1][:, here].T / 16.0
         copies[:, 3:69] = one[:, 3:69]
         copies[:, COPY0 : COPY0 + 2] = one[:, 3:5]
         copies[:, COPY0 + 2 : COPY0 + 4] = one[:, 67:69]
-        parts.append(copies)
         column_sum, row_sum = np.zeros((1, LANES)), np.zeros((1, LANES))
         for l in (5, 6, 7):
             w, f = FLATW[l], FLAT0[l]
             local = rows_of(down[l], l, t, -1, w - 2)[:, here]
             flat = np.zeros((BLOCK, LANES))
-            flat[:, f : f + w] = local.T
-            parts.append(flat)
+            flat[:, f : f + w] = local.T / 16.0**l
+            parts[l] = flat
             total_of = local.sum(axis=1)
             column_sum[0, f : f + w * w] = np.tile(total_of, w)
             row_sum[0, f : f + w * w] = np.repeat(total_of, w)
-        mats.append(np.concatenate(parts))
+        high = {l: part.astype(ml_dtypes.bfloat16) for l, part in parts.items()}
+        low = {l: (part - high[l].astype(np.float64)).astype(ml_dtypes.bfloat16) for l, part in parts.items()}
+        copies = np.concatenate([copies, np.zeros_like(copies)]).astype(ml_dtypes.bfloat16)
+        blocks = [np.concatenate([high[1], copies], axis=1), np.concatenate([low[1], np.zeros_like(copies)], axis=1)]
+        blocks += [np.concatenate([high[l], low[l]], axis=1) for l in range(2, 8)]
+        mats.append(np.concatenate(blocks))
 
         expand_a, expand_b = np.zeros((LANES, BLOCK)), np.zeros((LANES, BLOCK))
         row_a, row_b = np.zeros((BLOCK, LANES)), np.zeros((BLOCK, LANES))
@@ -129,11 +133,6 @@
                 [row_a, row_b, spread_rows.reshape(-1, LANES), np.repeat(weight_of[:, None], LANES, 1), np.repeat(row_sum, 8, 0)]
             )
         )
-    mats = np.stack(mats).astype(np.float32)
-    high = mats.astype(ml_dtypes.bfloat16)
-    low = (mats - high.astype(np.float32)).astype(ml_dtypes.bfloat16)
-    split = np.stack([high, low], axis=1)
-
     flat = np.zeros((2, LANES, LANES))
     for which, l in ((0, 7), (1, 6)):
         w, v = FLATW[l], FLATW[l - 1]
@@ -144,14 +143,14 @@
                 local[i, j + 1] += weight
         kron = np.einsum("ai,bj->ijab", local, local).reshape(w * w, v * v)
         flat[which, FLAT0[l] : FLAT0[l] + w * w, FLAT0[l - 1] : FLAT0[l - 1] + v * v] = kron
-    return split, np.stack(cols).astype(np.float32), np.stack(rows).astype(np.float32), flat.astype(np.float32)
-
-
-MATS, COLS, ROWC, FLAT = tile_constants()
-N_MATS, N_COLS, N_ROWC = MATS.shape[2], COLS.shape[1], ROWC.shape[1]
-COPY_AT = 1024
-FLAT_AT = {5: 1152, 6: 1280, 7: 1408}
-SPREAD_AT, WEIGHT_AT, RSUM_AT = 256, 808, 936
+    cols = [np.concatenate([part, flat[0], flat[1]]) for part in cols]
+    return np.stack(mats), np.stack(cols).astype(np.float32), np.stack(rows).astype(np.float32)
+
+
+MATS, COLS, ROWC = tile_constants()
+N_MATS, N_COLS, N_ROWC = MATS.shape[1], COLS.shape[1], ROWC.shape[1]
+MATS_AT = {1: 0, 2: 512, 3: 768, 4: 1024, 5: 1280, 6: 1408, 7: 1536}
+SPREAD_AT, WEIGHT_AT, RSUM_AT, FLAT_AT = 256, 808, 936, 264
 
 BEYOND = (1, -1, 2, -2, 3, -3)
 AROUND = [(a, b) for a in (-1, 0, 1) for b in (-1, 0, 1) if a or b]
@@ -160,14 +159,17 @@
 SIDE_TILES = -(-len(ITEMS) // 16)
 
 
-def split_dot(a, mat_ref, at, depth, exact=False):
+def split(a):
     high = a.astype(jnp.bfloat16)
-    low = (a - high.astype(F32)).astype(jnp.bfloat16)
-    m_high = mat_ref[0, at : at + depth, :]
-    out = jnp.dot(high, m_high, preferred_element_type=F32) + jnp.dot(low, m_high, preferred_element_type=F32)
-    if not exact:
-        out = out + jnp.dot(high, mat_ref[1, at : at + depth, :], preferred_element_type=F32)
-    return out
+    return high, (a - high.astype(F32)).astype(jnp.bfloat16)
+
+
+def split_dot(a, mats, l, depth):
+    high, low = split(a)
+    at = MATS_AT[l]
+    both = jnp.dot(high, mats[at : at + depth, :], preferred_element_type=F32)
+    rest = jnp.dot(low, mats[at : at + depth, :LANES], preferred_element_type=F32)
+    return both[:, :LANES] + both[:, LANES:] + rest
 
 
 def lanes_in(low, high, shape=(1, LANES)):
@@ -187,10 +189,10 @@
 def make_kernel(nr, nc):
     cells = float(nr * nc)
 
-    def kernel(bits_ref, label_ref, x_hbm, mats_hbm, cols_hbm, rows_hbm, flat_hbm, out_ref, *scratch):
-        (x_ref, mats, cols, rowc, flat, s1, s2, s3, s4, s5, s6, s7, e1, e2, e3, e4, d1, d2, d3, d4, copies_ref, xs_ref,
+    def kernel(bits_ref, label_ref, x_hbm, mats_hbm, cols_hbm, rows_hbm, out_ref, *scratch):
+        (x_ref, mats, cols, rowc, s1, s2, s3, s4, s5, s6, s7, e1, e2, e3, e4, d1, d2, d3, d4, copies_ref, xs_ref,
          planes, ones_ref, m_send, m_col, m_row, mask_send, mask_recv, t_send, t_row, t_col, v_send, v_recv, h_send,
-         h_recv, w_ref, load_sem, send_sem, recv_sem) = scratch
+         h_recv, c_send, c_recv, lines_ref, w_ref, load_sem, send_sem, recv_sem, far_sem) = scratch
         s = {1: s1, 2: s2, 3: s3, 4: s4, 5: s5, 6: s6, 7: s7}
         e = {1: e1, 2: e2, 3: e3, 4: e4}
         d = {1: d1, 2: d2, 3: d3, 4: d4}
@@ -209,35 +211,53 @@
             return ok.astype(jnp.int32).astype(F32)
 
         row_place, col_place = place(r, nr), place(c_at, nc)
+        part = V * C * BLOCK // 8
         loads = [
-            pltpu.make_async_copy(x_hbm, x_ref, load_sem.at[0]),
-            pltpu.make_async_copy(rows_hbm.at[row_place], rowc, load_sem.at[1]),
-            pltpu.make_async_copy(cols_hbm.at[col_place], cols, load_sem.at[2]),
-            pltpu.make_async_copy(mats_hbm.at[col_place], mats, load_sem.at[3]),
-            pltpu.make_async_copy(flat_hbm, flat, load_sem.at[4]),
+            pltpu.make_async_copy(
+                rows_hbm.at[row_place, WEIGHT_AT : WEIGHT_AT + BLOCK], rowc.at[WEIGHT_AT : WEIGHT_AT + BLOCK], load_sem.at[0]
+            ),
+            pltpu.make_async_copy(cols_hbm.at[col_place, :FLAT_AT], cols.at[:FLAT_AT], load_sem.at[1]),
+            pltpu.make_async_copy(mats_hbm.at[col_place], mats, load_sem.at[2]),
+            pltpu.make_async_copy(rows_hbm.at[row_place, :WEIGHT_AT], rowc.at[:WEIGHT_AT], load_sem.at[3]),
+            pltpu.make_async_copy(
+                rows_hbm.at[row_place, WEIGHT_AT + BLOCK :], rowc.at[WEIGHT_AT + BLOCK :], load_sem.at[4]
+            ),
+            pltpu.make_async_copy(cols_hbm.at[col_place, FLAT_AT:], cols.at[FLAT_AT:], load_sem.at[5]),
         ]
-        for load in loads:
+        image_loads = [
+            pltpu.make_async_copy(
+                x_hbm.at[i * part : (i + 1) * part], x_ref.at[i * part : (i + 1) * part], load_sem.at[6 + i // 4]
+            )
+            for i in range(8)
+        ]
+        barrier = pltpu.get_barrier_semaphore()
+        partners = [(0, i) for i in range(1, nc)] + [(i, 0) for i in (1, -1, 2, -2, 3, -3, 4, -4)]
+        partners += [(a, b) for a, b in AROUND if a and b]
+        loads[0].start()
+        loads[1].start()
+        for load in image_loads:
             load.start()
-
-        barrier = pltpu.get_barrier_semaphore()
-        partners = [(0, i) for i in range(1, nc)] + [(i, 0) for i in range(1, nr)]
-        partners += [(a, b) for a, b in AROUND if a and b]
+        for load in loads[2:]:
+            load.start()
         for a, b in partners:
             pl.semaphore_signal(barrier, inc=1, device_id=device(a, b), device_id_type=MESH)
 
-        used = [0]
-        sent = []
-
-        def post(src, dst, to):
-            slot = used[0]
-            used[0] += 1
-            copy = pltpu.make_async_remote_copy(
-                src_ref=src, dst_ref=dst, send_sem=send_sem.at[slot], recv_sem=recv_sem.at[slot],
-                device_id=device(*to), device_id_type=MESH,
-            )
-            copy.start()
-            sent.append(copy)
-            return copy
+        groups = []
+
+        def post(whole, copies):
+            slot = len(groups)
+
+            def describe(src, dst, to):
+                return pltpu.make_async_remote_copy(
+                    src_ref=src, dst_ref=dst, send_sem=send_sem.at[slot], recv_sem=recv_sem.at[slot],
+                    device_id=device(*to), device_id_type=MESH,
+                )
+
+            for src, dst, to in copies:
+                describe(src, dst, to).start()
+            group = describe(whole, whole, copies[0][2])
+            groups.append(group)
+            return group
 
         view = lax.broadcasted_iota(jnp.int32, (V, LANES), 0)
         lane = lax.broadcasted_iota(jnp.int32, (V, LANES), 1)
@@ -253,28 +273,30 @@
             s[l][n + 6 :] = jnp.zeros((s[l].shape[0] - n - 6, 24, LANES), F32)
         for l in range(1, 5):
             e[l][SIDE[l] + 9 :] = jnp.zeros((ROWS[l] - SIDE[l] - 9, 24, LANES), F32)
-        w_ref[...] = jnp.zeros_like(w_ref)
+        for l, n in ((1, 75), (2, 42), (3, 25), (4, 17)):
+            d[l][n:] = jnp.zeros((ROWS[l] - n, 24, LANES), F32)
+        copies_ref[75:] = jnp.zeros((5, 24, LANES), F32)
+        lines_ref[...] = jnp.zeros_like(lines_ref)
 
         loads[0].wait()
         loads[1].wait()
-        loads[2].wait()
 
         weight_rows = rowc[WEIGHT_AT : WEIGHT_AT + BLOCK, :]
         weight_cols = cols[256 + 7 : 256 + 8, :]
+        parts = [[] for _ in range(C)]
+        for v in range(V):
+            if v % 4 == 0:
+                for load in image_loads[v : v + 4]:
+                    load.wait()
+            for c in range(C):
+                weighted = x_ref[(v * C + c) * BLOCK : (v * C + c + 1) * BLOCK, :] * weight_rows
+                parts[c].append(jnp.sum(weighted.reshape(16, 8, LANES), axis=0)[None])
         mean = jnp.zeros((1, LANES), F32)
         for c in range(C):
-            parts = []
-            for v in range(V):
-                weighted = x_ref[(v * C + c) * BLOCK : (v * C + c + 1) * BLOCK, :] * weight_rows
-                parts.append(jnp.sum(weighted.reshape(16, 8, LANES), axis=0)[None])
-            both = jnp.sum(jnp.concatenate(parts, axis=0), axis=1) * weight_cols
+            both = jnp.sum(jnp.concatenate(parts[c], axis=0), axis=1) * weight_cols
             total = jnp.sum(both, axis=1, keepdims=True)
             mean = mean + jnp.sum(jnp.where(lane == view + V * c, total, 0.0), axis=0, keepdims=True)
         m_send[0] = mean * (1.0 / cells)
-
-        pl.semaphore_wait(barrier, len(partners))
-        m_cols = [post(m_send.at[0], m_col.at[i - 1], (0, i)) for i in range(1, nc)]
-        masks = [post(mask_send, mask_recv.at[i], to) for i, to in enumerate(AROUND)]
 
         def pixel_row(row):
             return jnp.concatenate(
@@ -286,9 +308,12 @@
             for a, w in zip(range(-2, 3), (1.0, 4.0, 6.0, 4.0, 1.0)):
                 term = get(2 * k + a)
                 if term is not None:
-                    term = term * (w / 16.0)
+                    term = term * w
                     total = term if total is None else total + term
             return total
+
+        def five_taps(x):
+            return (x[0] + x[4]) + 4.0 * (x[1] + x[3]) + 6.0 * x[2]
 
         def edge_row(row):
             return pixel_row(row) if 0 <= row < BLOCK else None
@@ -299,11 +324,7 @@
         def first_pair(i, carry):
             rows = [pixel_row(4 * i + j) for j in range(7)]
             for half in range(2):
-                total = None
-                for j, w in enumerate((1.0, 4.0, 6.0, 4.0, 1.0)):
-                    term = rows[2 * half + j] * (w / 16.0)
-                    total = term if total is None else total + term
-                s1[2 * i + half + 5] = total
+                s1[2 * i + half + 5] = five_taps(rows[2 * half :])
             return carry
 
         lax.fori_loop(0, 31, first_pair, 0)
@@ -324,11 +345,7 @@
             src, dst = s[l - 1], s[l]
 
             def one(i, src=src, dst=dst):
-                total = None
-                for j, w in enumerate((1.0, 4.0, 6.0, 4.0, 1.0)):
-                    term = src[2 * i + j] * (w / 16.0)
-                    total = term if total is None else total + term
-                dst[i + 3] = total
+                dst[i + 3] = five_taps([src[2 * i + j] for j in range(5)])
 
             if l == 2:
                 def five(i, carry, one=one):
@@ -342,25 +359,31 @@
                     one(i)
             trim(l)
 
-        loads[3].wait()
-        loads[4].wait()
+        for load in loads[2:]:
+            load.wait()
         tops = jnp.zeros((24, LANES), F32)
         for l in (5, 6, 7):
             w = FLATW[l]
-            flat_l = split_dot(s[l][3 : 3 + w].reshape(w * 24, LANES), mats, FLAT_AT[l], BLOCK).reshape(w, 24, LANES)
+            flat_l = split_dot(s[l][3 : 3 + w].reshape(w * 24, LANES), mats, l, BLOCK).reshape(w, 24, LANES)
             for i in range(w):
                 tops = tops + turn(flat_l[i], i * w)
         t_send[0, 0:24] = tops
         t_send[0, 24:32] = own_mask * (rowc[RSUM_AT : RSUM_AT + 1, :] * cols[256 + 6 : 256 + 7, :])
-        t_rows = [post(t_send.at[0], t_row.at[i], (off, 0)) for i, off in enumerate(BEYOND)]
+
+        pl.semaphore_wait(barrier, len(partners))
+        for away in (4, -4):
+            pl.semaphore_signal(far_sem, inc=1, device_id=device(away, 0), device_id_type=MESH)
+        m_cols = post(m_col, [(m_send.at[0], m_col.at[i - 1], (0, i)) for i in range(1, nc)])
+        masks = post(mask_recv, [(mask_send, mask_recv.at[i], to) for i, to in enumerate(AROUND)])
+        t_rows = post(t_row, [(t_send.at[0], t_row.at[i], (off, 0)) for i, off in enumerate(BEYOND)])
 
         for l in range(1, 5):
             n, src, dst = SIDE[l], s[l + 1], e[l]
 
             def pair(i, src=src, dst=dst):
                 x0, x1, x2 = src[i + 1], src[i + 2], src[i + 3]
-                dst[2 * i] = (x0 + x2) * 0.125 + x1 * 0.75
-                return (x1 + x2) * 0.5
+                dst[2 * i] = (x0 + x2) + 6.0 * x1
+                return 4.0 * (x1 + x2)
 
             half = n // 2 + 4
             if l < 3:
@@ -373,29 +396,30 @@
             else:
                 for i in range(half):
                     dst[2 * i + 1] = pair(i)
-            dst[n + 8] = (src[half + 1] + src[half + 3]) * 0.125 + src[half + 2] * 0.75
-
-        chunk = {1: 16, 2: 16, 3: 16, 4: 24}
-        for l in range(1, 5):
-            m = chunk[l]
+            dst[n + 8] = (src[half + 1] + src[half + 3]) + 6.0 * src[half + 2]
+
+        for l, m, times in ((1, 15, 5), (2, 14, 3), (3, 25, 1), (4, 17, 1)):
 
             def details(i, carry, l=l, m=m):
-                at = pl.multiple_of(i * m, m)
+                at = i * m
                 both = jnp.concatenate(
                     [s[l][pl.ds(at, m)].reshape(m * 24, LANES), e[l][pl.ds(at, m)].reshape(m * 24, LANES)], axis=1
                 )
-                d[l][pl.ds(at, m)] = split_dot(both, mats, 256 * (l - 1), 256).reshape(m, 24, LANES)
-                if l == 1:
-                    only = split_dot(both[:, :LANES], mats, COPY_AT, BLOCK, exact=True)
-                    copies_ref[pl.ds(at, m)] = only.reshape(m, 24, LANES)
+                if l > 1:
+                    d[l][pl.ds(at, m)] = split_dot(both, mats, l, 256).reshape(m, 24, LANES)
+                else:
+                    high, low = split(both)
+                    wide = jnp.dot(high, mats[0:256, :], preferred_element_type=F32)
+                    wide = wide + jnp.dot(low, mats[0:256, :], preferred_element_type=F32)
+                    rest = jnp.dot(high, mats[256:512, :LANES], preferred_element_type=F32)
+                    d[l][pl.ds(at, m)] = (wide[:, :LANES] + rest).reshape(m, 24, LANES)
+                    copies_ref[pl.ds(at, m)] = wide[:, LANES:].reshape(m, 24, LANES)
                 return carry
 
-            lax.fori_loop(0, ROWS[l] // m, details, 0)
-
-        for copy in m_cols:
-            copy.wait_recv()
-        m_send[1] = m_send[0] + jnp.sum(m_col[...], axis=0)
-        m_rows = [post(m_send.at[1], m_row.at[i - 1], (i, 0)) for i in range(1, nr)]
+            if times > 1:
+                lax.fori_loop(0, times, details, 0)
+            else:
+                details(0, 0)
 
         def weights(mask):
             total = jnp.sum(mask, axis=0, keepdims=True)
@@ -428,13 +452,16 @@
                 total = total + moved * (inside(step, 0) if stride == "row" else inside(0, step))
             return total
 
-        for copy in t_rows:
-            copy.wait_recv()
+        t_rows.wait_recv()
         t_send[1] = gather_tops(t_send[0], t_row, "row", r)
-        t_cols = [post(t_send.at[1], t_col.at[i], (0, off)) for i, off in enumerate(BEYOND)]
-
-        for copy in masks:
-            copy.wait_recv()
+        t_cols = post(t_col, [(t_send.at[1], t_col.at[i], (0, off)) for i, off in enumerate(BEYOND)])
+
+        m_cols.wait_recv()
+        pl.semaphore_wait(far_sem, 2)
+        m_send[1] = m_send[0] + jnp.sum(m_col[...], axis=0)
+        m_rows = post(m_row, [(m_send.at[1], m_row.at[i - 1], (i, 0)) for i in range(1, nr)])
+
+        masks.wait_recv()
         around = {(0, 0): own_mask}
         for i, (a, b) in enumerate(AROUND):
             around[(-a, -b)] = mask_recv[i] * inside(-a, -b)
@@ -474,20 +501,44 @@
 
             lax.fori_loop(0, ROWS[l] // 8, blend, 0)
 
+        for w in range(2):
+            corners = [jnp.zeros((8, LANES), F32) for _ in range(2)]
+            for c in range(C):
+                at = {l: ROW0[l] + (SIDE[l] + 3 if w else 0) for l in range(1, 5)}
+                halves = [planes[c, at[l] : at[l] + 8] + planes[c, at[l + 1] : at[l + 1] + 8] for l in (1, 3)]
+                one = copies_ref[at[1] : at[1] + 8, V * c : V * c + V, :]
+                one = jnp.sum(one * row_weights[1 if w else -1][None], axis=1)
+                v_send[w, c, 0] = halves[0] - keep(one, 0, COPY0)
+                v_send[w, c, 1] = halves[1]
+                for side in range(2):
+                    for l in range(1, 5):
+                        slot = 8 * (4 * c + l - 1)
+                        first = LANE0[l] + (SIDE[l] + 3 if side else 0)
+                        corners[side] += keep(turn(halves[HALF[l]], slot - first), slot, slot + 6)
+                    slot, first = (32 * c, COPY0 + 2) if side else (32 * c + 3, COPY0)
+                    corners[side] -= keep(turn(one, slot - first), slot, slot + 2)
+            for side in range(2):
+                c_send[2 * w + side] = corners[side]
+        v_rims = post(v_recv, [(v_send.at[w], v_recv.at[w], (2 * w - 1, 0)) for w in range(2)])
+        ends = [(i, 2 * (i // 2) - 1, 2 * (i % 2) - 1) for i in range(4)]
+        c_rims = post(c_recv, [(c_send.at[i], c_recv.at[i], (a, b)) for i, a, b in ends])
+        for which in range(2):
+            for g in range(SIDE_TILES):
+                tile = jnp.zeros((8, LANES), F32)
+                for u, (c, l, row) in enumerate(ITEMS[16 * g : 16 * g + 16]):
+                    first = LANE0[l] + (SIDE[l] + 3 if which else 0)
+                    tile = tile + keep(turn(planes[c, row : row + 8], 8 * u - first), 8 * u, 8 * u + 6)
+                    if l == 1:
+                        slot, first = (8 * u, COPY0 + 2) if which else (8 * u + 3, COPY0)
+                        tile = tile - keep(turn(ones_ref[c, row : row + 8], slot - first), slot, slot + 2)
+                h_send[which, g] = tile
+        h_rims = post(h_recv, [(h_send.at[w], h_recv.at[w], (0, 2 * w - 1)) for w in range(2)])
         for c in range(C):
-            v_send[0, c, 0] = planes[c, 0:8] + planes[c, 80:88]
-            v_send[0, c, 1] = planes[c, 128:136] + planes[c, 160:168]
-            part = copies_ref[0:8, V * c : V * c + V, :]
-            v_send[0, c, 2] = jnp.sum(part * row_weights[-1][None], axis=1)
-            v_send[1, c, 0] = planes[c, 67:75] + planes[c, 115:123]
-            v_send[1, c, 1] = planes[c, 147:155] + planes[c, 171:179]
-            part = copies_ref[67:75, V * c : V * c + V, :]
-            v_send[1, c, 2] = jnp.sum(part * row_weights[1][None], axis=1)
-        v_rows = [post(v_send.at[0], v_recv.at[0], (-1, 0)), post(v_send.at[1], v_recv.at[1], (1, 0))]
-
-        for copy in t_cols:
-            copy.wait_recv()
+            planes[c, 0:80] -= keep(ones_ref[c], 0, COPY0)
+
+        t_cols.wait_recv()
         tops_all = gather_tops(t_send[1], t_col, "col", c_at)
+        flat = [cols[FLAT_AT : FLAT_AT + LANES], cols[FLAT_AT + LANES : FLAT_AT + 2 * LANES]]
         images, mask = tops_all[0:24], tops_all[24:32]
         whole = jnp.sum(mask, axis=0, keepdims=True)
         here = whole > 0.0
@@ -500,54 +551,43 @@
         for which in range(2):
             step = jnp.dot(chain, flat[which], precision=lax.Precision.HIGHEST, preferred_element_type=F32)
             chain = chain + jnp.where(here, step, 0.0)
+
         for c in range(C):
-            w_ref[V * c : V * c + V] = chain[8:16]
-
-        for copy in v_rows:
-            copy.wait_recv()
-        for which, away in ((1, -1), (0, 1)):
-            flag = inside(away, 0)
+            planes[c, ROW5 + 7 : ROW5 + 8] = jnp.zeros((1, LANES), F32)
+        for i in range(7):
+            line = keep(turn(chain, LANE5 - 7 * i), LANE5, LANE5 + 7)
+            for c in range(C):
+                planes[c, ROW5 + i : ROW5 + i + 1] = line[c : c + 1]
+            for v in range(V):
+                lines_ref[8 * v + i : 8 * v + i + 1] = line[8 + v : 9 + v]
+        wide = jnp.dot(lines_ref[...], cols[128:256], precision=lax.Precision.HIGH, preferred_element_type=F32)
+        for v in range(V):
+            w_ref[v] = jnp.dot(
+                rowc[128:256, 56:64], wide[8 * v : 8 * v + 8], precision=lax.Precision.HIGH, preferred_element_type=F32
+            )
+
+        v_rims.wait_recv()
+        c_rims.wait_recv()
+        h_rims.wait_recv()
+        for w, a in ((1, -1), (0, 1)):
+            flag = inside(a, 0)
             for c in range(C):
                 for l in range(1, 5):
-                    at = ROW0[l] + (3 if away < 0 else SIDE[l])
-                    low = LANE0[l]
-                    got = v_recv[which, c, HALF[l]][0:6] * flag
+                    at, low = ROW0[l] + (3 if a < 0 else SIDE[l]), LANE0[l]
+                    got = v_recv[w, c, HALF[l]][0:6] * flag
                     planes[c, at : at + 6] += keep(got, low, low + SIDE[l] + 9)
-                at = 3 if away < 0 else SIDE[1]
-                ones_ref[c, at : at + 6] += v_recv[which, c, 2][0:6] * flag
-        for which in range(2):
-            for g in range(SIDE_TILES):
-                tile = jnp.zeros((8, LANES), F32)
-                for u, (c, l, row) in enumerate(ITEMS[16 * g : 16 * g + 16]):
-                    first = LANE0[l] + (SIDE[l] + 3 if which else 0)
-                    tile = tile + keep(turn(planes[c, row : row + 8], 8 * u - first), 8 * u, 8 * u + 6)
-                    if l == 1:
-                        slot, first = (8 * u, COPY0 + 2) if which else (8 * u + 3, COPY0)
-                        tile = tile - keep(turn(ones_ref[c, row : row + 8], slot - first), slot, slot + 2)
-                h_send[which, g] = tile
-        h_cols = [post(h_send.at[0], h_recv.at[0], (0, -1)), post(h_send.at[1], h_recv.at[1], (0, 1))]
-
-        for c in range(C):
-            planes[c, 0:80] -= keep(ones_ref[c], 0, COPY0)
-            planes[c, ROW5 : ROW5 + 8] = jnp.zeros((8, LANES), F32)
-
-        for copy in m_rows:
-            copy.wait_recv()
-        means = m_send[1] + jnp.sum(m_row[...], axis=0)
-        picked = jnp.where(lane // V == view, jnp.broadcast_to(means, (V, LANES)), 0.0)
-        level5 = chain[0:8] + jnp.dot(picked, w_ref[...], precision=lax.Precision.HIGHEST, preferred_element_type=F32)
-        for i in range(7):
-            line = keep(turn(level5, LANE5 - 7 * i), LANE5, LANE5 + 7)
-            for c in range(C):
-                planes[c, ROW5 + i : ROW5 + i + 1] = line[c : c + 1]
-
-        for copy in h_cols:
-            copy.wait_recv()
-        for which, away in ((1, -1), (0, 1)):
-            flag = inside(0, away)
+            for side, b in ((1, -1), (0, 1)):
+                got = c_recv[2 * w + side][0:6] * inside(a, b)
+                for c in range(C):
+                    for l in range(1, 5):
+                        at, slot = ROW0[l] + (3 if a < 0 else SIDE[l]), 8 * (4 * c + l - 1)
+                        first = LANE0[l] + (3 if b < 0 else SIDE[l])
+                        planes[c, at : at + 6] += keep(turn(got, first - slot), first, first + 6)
+        for which, b in ((1, -1), (0, 1)):
+            flag = inside(0, b)
             for i, (c, l, row) in enumerate(ITEMS):
                 u = i % 16
-                first = LANE0[l] + (3 if away < 0 else SIDE[l])
+                first = LANE0[l] + (3 if b < 0 else SIDE[l])
                 got = h_recv[which, i // 16] * flag
                 planes[c, row : row + 8] += keep(turn(got, first - 8 * u), first, first + 6)
 
@@ -556,10 +596,21 @@
             lower = jnp.dot(rowc[128:256, 0:64], planes[c, 128:192], precision=lax.Precision.HIGH, preferred_element_type=F32)
             total = jnp.dot(upper, cols[0:128], precision=lax.Precision.HIGH, preferred_element_type=F32)
             total = total + jnp.dot(lower, cols[128:256], precision=lax.Precision.HIGH, preferred_element_type=F32)
-            out_ref[c] = xs_ref[c] + total
-
-        for copy in sent:
-            copy.wait_send()
+            xs_ref[c] += total
+
+        m_rows.wait_recv()
+        means = m_send[1] + jnp.sum(m_row[...], axis=0)
+        each = [jnp.broadcast_to(means[:, i : i + 1], (8, LANES)) for i in range(V * C)]
+        for i in range(BLOCK // 8):
+            added = [w_ref[v, 8 * i : 8 * i + 8] for v in range(V)]
+            for c in range(C):
+                total = xs_ref[c, 8 * i : 8 * i + 8]
+                for v in range(V):
+                    total = total + each[V * c + v] * added[v]
+                out_ref[c, 8 * i : 8 * i + 8] = total
+
+        for group in groups:
+            group.wait_send()
 
     def vmem(*shape):
         return pltpu.VMEM(shape, F32)
@@ -568,10 +619,9 @@
     wides = [vmem(ROWS[l], 24, LANES) for l in range(1, 5)]
     scratch = [
         vmem(V * C * BLOCK, LANES),
-        pltpu.VMEM((2, N_MATS, LANES), jnp.bfloat16),
+        pltpu.VMEM((N_MATS, 2 * LANES), jnp.bfloat16),
         vmem(N_COLS, LANES),
         vmem(N_ROWC, LANES),
-        vmem(2, LANES, LANES),
         *slabs, *wides, *wides,
         vmem(80, 24, LANES),
         vmem(C, BLOCK, LANES),
@@ -585,22 +635,26 @@
         vmem(2, 32, LANES),
         vmem(6, 32, LANES),
         vmem(6, 32, LANES),
-        vmem(2, C, 3, 8, LANES),
-        vmem(2, C, 3, 8, LANES),
+        vmem(2, C, 2, 8, LANES),
+        vmem(2, C, 2, 8, LANES),
         vmem(2, SIDE_TILES, 8, LANES),
         vmem(2, SIDE_TILES, 8, LANES),
-        vmem(LANES, LANES),
-        pltpu.SemaphoreType.DMA((5,)),
-        pltpu.SemaphoreType.DMA((nr + nc + 22,)),
-        pltpu.SemaphoreType.DMA((nr + nc + 22,)),
+        vmem(4, 8, LANES),
+        vmem(4, 8, LANES),
+        vmem(8 * V, LANES),
+        vmem(V, BLOCK, LANES),
+        pltpu.SemaphoreType.DMA((8,)),
+        pltpu.SemaphoreType.DMA((8,)),
+        pltpu.SemaphoreType.DMA((8,)),
+        pltpu.SemaphoreType.REGULAR,
     ]
     return pl.pallas_call(
         kernel,
         out_shape=jax.ShapeDtypeStruct((C, BLOCK, BLOCK), F32),
-        in_specs=[pl.BlockSpec(memory_space=pltpu.SMEM)] * 2 + [pl.BlockSpec(memory_space=pl.ANY)] * 5,
+        in_specs=[pl.BlockSpec(memory_space=pltpu.SMEM)] * 2 + [pl.BlockSpec(memory_space=pl.ANY)] * 4,
         out_specs=pl.BlockSpec(memory_space=pltpu.VMEM),
         scratch_shapes=scratch,
-        compiler_params=pltpu.CompilerParams(collective_id=0, has_side_effects=True, vmem_limit_bytes=48 << 20),
+        compiler_params=pltpu.CompilerParams(collective_id=0, has_side_effects=True, vmem_limit_bytes=54500 << 10),
     )
 
 
@@ -611,7 +665,7 @@
         planes = view_images.reshape(V * C * BLOCK, BLOCK)
         return call(
             intersection_bits, seam_labels, planes,
-            jnp.asarray(MATS), jnp.asarray(COLS), jnp.asarray(ROWC), jnp.asarray(FLAT),
+            jnp.asarray(MATS), jnp.asarray(COLS), jnp.asarray(ROWC),
         )
 
     placed = (P(None, None, "row", "col"), P("row", "col"), P("row", "col"))

time: 43 us -> 31.1 us (0.72)
  Pallas kernels: 35.6 us -> 29 us
  local copies, waits for them, and re-layouts: 5.76 us -> 0.68 us
    pallas_call x1, Pallas kernels: 35.6 us -> 29 us  [local(): call(intersection_bits, seam_labels, planes, jnp.asarray(MATS), jnp.asarr...]
    unnamed x9 -> x1, local copies, waits for them, and re-layouts: 5.76 us -> 0.68 us
where the time goes in v2:
time: 31.1 us; the launch traced here: 30.9 us
  Pallas kernels  29 us (93%)
  between operations  1.3 us (4%)
  local copies, waits for them, and re-layouts  0.68 us (2%)
    pallas_call x1, Pallas kernels, local(): call(intersection_bits, seam_labels, planes, jnp.asarray(MATS), jnp.asarr...  29 us
    unnamed x1, local copies, waits for them, and re-layouts  0.68 us

profile of v2, /device:TPU:1, one launch (start us, length us, event | category | flops | bytes accessed | tf_op | source)
XLA Modules:
  0.0 30.9 jit_solution(12168441081997118995)
XLA Ops:
  1.3 29.0 %shard_map.64 = f32[3,128,128]{2,1,0:T(8,128)S(1)} custom-call(s32[1,1]{1,0:T(1,128)S(6)} %copy.8.bits_ref, s32[1,1]{1,0:T(1,128)S(6)} %copy.9.label_ref, f32[3072,128]{1,0:T(8,128)} %bitcast.1, bf16[5,1664,256]{2,1,0:T(8,128)(2,1)} %constant.6.clone.mats_hbm, f32[5,520,128]{2,1,0:T(8,128)} %constant.7.clone.cols_hbm, f32[5,944,128]{2,1,0:T(8,128)} %constant.8.clone.rows_hbm), custom_call_target="tpu_custom_call" | custom-call | tf_op jit(solution)/shard_map/pallas_call | solution.py:666
  30.3 0.7 %copy.10 = f32[3,128,128]{2,1,0:T(8,128)} copy(f32[3,128,128]{2,1,0:T(8,128)S(1)} %shard_map.64) | data formatting | bytes 393216

commit v3 on v2

--- a/solution.py
+++ b/solution.py
@@ -152,10 +152,9 @@
 MATS_AT = {1: 0, 2: 512, 3: 768, 4: 1024, 5: 1280, 6: 1408, 7: 1536}
 SPREAD_AT, WEIGHT_AT, RSUM_AT, FLAT_AT = 256, 808, 936, 264
 
-BEYOND = (1, -1, 2, -2, 3, -3)
 AROUND = [(a, b) for a in (-1, 0, 1) for b in (-1, 0, 1) if a or b]
 ITEMS = [(c, l, ROW0[l] + 8 * i) for c in range(C) for l in range(1, 5) for i in range(ROWS[l] // 8)]
-ITEMS = [item for item in ITEMS if item[2] - ROW0[item[1]] < SIDE[item[1]] + 9]
+ITEMS = [item for item in ITEMS if item[2] - ROW0[item[1]] <= SIDE[item[1]] + 5]
 SIDE_TILES = -(-len(ITEMS) // 16)
 
 
@@ -191,7 +190,7 @@
 
     def kernel(bits_ref, label_ref, x_hbm, mats_hbm, cols_hbm, rows_hbm, out_ref, *scratch):
         (x_ref, mats, cols, rowc, s1, s2, s3, s4, s5, s6, s7, e1, e2, e3, e4, d1, d2, d3, d4, copies_ref, xs_ref,
-         planes, ones_ref, m_send, m_col, m_row, mask_send, mask_recv, t_send, t_row, t_col, v_send, v_recv, h_send,
+         planes, ones_ref, m_send, m_col, m_row, mask_send, mask_recv, t_send, t_packed, t_last, t_row, tp_row, tl_row, t_col, tp_col, tl_col, v_send, v_recv, h_send,
          h_recv, c_send, c_recv, lines_ref, w_ref, load_sem, send_sem, recv_sem, far_sem) = scratch
         s = {1: s1, 2: s2, 3: s3, 4: s4, 5: s5, 6: s6, 7: s7}
         e = {1: e1, 2: e2, 3: e3, 4: e4}
@@ -359,6 +358,12 @@
                     one(i)
             trim(l)
 
+        pl.semaphore_wait(barrier, len(partners))
+        for away in (4, -4):
+            pl.semaphore_signal(far_sem, inc=1, device_id=device(away, 0), device_id_type=MESH)
+        m_cols = post(m_col, [(m_send.at[0], m_col.at[i - 1], (0, i)) for i in range(1, nc)])
+        masks = post(mask_recv, [(mask_send, mask_recv.at[i], to) for i, to in enumerate(AROUND)])
+
         for load in loads[2:]:
             load.wait()
         tops = jnp.zeros((24, LANES), F32)
@@ -370,12 +375,29 @@
         t_send[0, 0:24] = tops
         t_send[0, 24:32] = own_mask * (rowc[RSUM_AT : RSUM_AT + 1, :] * cols[256 + 6 : 256 + 7, :])
 
-        pl.semaphore_wait(barrier, len(partners))
-        for away in (4, -4):
-            pl.semaphore_signal(far_sem, inc=1, device_id=device(away, 0), device_id_type=MESH)
-        m_cols = post(m_col, [(m_send.at[0], m_col.at[i - 1], (0, i)) for i in range(1, nc)])
-        masks = post(mask_recv, [(mask_send, mask_recv.at[i], to) for i, to in enumerate(AROUND)])
-        t_rows = post(t_row, [(t_send.at[0], t_row.at[i], (off, 0)) for i, off in enumerate(BEYOND)])
+        def post_tops(value, recv, packed_recv, last_recv, hop):
+            t_send[hop] = value
+            packed = jnp.zeros((V, LANES), F32)
+            last = jnp.zeros((V, LANES), F32)
+            for j in range(4):
+                tile = value[V * j : V * j + V]
+                if j < 3:
+                    packed = packed + keep(turn(tile, 41 * j - FLAT0[6]), 41 * j, 41 * j + 41)
+                last = last + keep(turn(tile, 16 * j - FLAT0[7]), 16 * j, 16 * j + 16)
+            t_packed[hop, 0:8] = packed
+            t_packed[hop, 8:16] = value[24:32]
+            t_last[hop] = last
+
+            def to(step):
+                return (step, 0) if hop == 0 else (0, step)
+
+            return [
+                post(recv, [(t_send.at[hop], recv.at[i], to(step)) for i, step in enumerate((1, -1))]),
+                post(packed_recv, [(t_packed.at[hop], packed_recv.at[i], to(step)) for i, step in enumerate((2, -2))]),
+                post(last_recv, [(t_last.at[hop], last_recv.at[i], to(step)) for i, step in enumerate((3, -3))]),
+            ]
+
+        t_rows = post_tops(t_send[0], t_row, tp_row, tl_row, 0)
 
         for l in range(1, 5):
             n, src, dst = SIDE[l], s[l + 1], e[l]
@@ -425,36 +447,35 @@
             total = jnp.sum(mask, axis=0, keepdims=True)
             return mask / jnp.where(total > 0.0, total, 1.0)
 
-        own_weights = weights(own_mask)
-        for c in range(C):
-            total = None
-            for v in range(V):
-                term = x_ref[(v * C + c) * BLOCK : (v * C + c + 1) * BLOCK, :] * own_weights[v : v + 1, :]
-                total = term if total is None else total + term
-            xs_ref[c] = total
-
-        def gather_tops(own, recv, stride, at):
+        def gather_tops(own, recv, packed_recv, last_recv, stride):
             total = own
-            for i, off in enumerate(BEYOND):
-                got = recv[i]
-                step = -off
-                moved = None
-                for l in (5, 6, 7):
-                    w, n, f = FLATW[l], SIDE[l], FLAT0[l]
-                    if w <= n * abs(step):
-                        continue
-                    index = lax.broadcasted_iota(jnp.int32, (1, LANES), 1) - f
-                    along = index // w if stride == "row" else index % w
-                    ok = lanes_in(f, f + w * w)
-                    ok = jnp.logical_and(ok, jnp.logical_and(along - n * step >= 0, along - n * step < w))
-                    term = jnp.where(ok, turn(got, n * step * (w if stride == "row" else 1)), 0.0)
-                    moved = term if moved is None else moved + term
-                total = total + moved * (inside(step, 0) if stride == "row" else inside(0, step))
+            for i in range(2):
+                for far in (1, 2, 3):
+                    step = far if i else -far
+                    if far == 1:
+                        got = recv[i]
+                    elif far == 2:
+                        tiles = [turn(packed_recv[i, 0:8], FLAT0[6] - 41 * j) for j in range(3)]
+                        got = jnp.concatenate(tiles + [packed_recv[i, 8:16]], axis=0)
+                    else:
+                        got = jnp.concatenate([turn(last_recv[i], FLAT0[7] - 16 * j) for j in range(4)], axis=0)
+                    moved = None
+                    for l in (5, 6, 7):
+                        w, n, f = FLATW[l], SIDE[l], FLAT0[l]
+                        if w <= n * far:
+                            continue
+                        index = lax.broadcasted_iota(jnp.int32, (1, LANES), 1) - f
+                        along = index // w if stride == "row" else index % w
+                        ok = lanes_in(f, f + w * w)
+                        ok = jnp.logical_and(ok, jnp.logical_and(along - n * step >= 0, along - n * step < w))
+                        term = jnp.where(ok, turn(got, n * step * (w if stride == "row" else 1)), 0.0)
+                        moved = term if moved is None else moved + term
+                    total = total + moved * (inside(step, 0) if stride == "row" else inside(0, step))
             return total
 
-        t_rows.wait_recv()
-        t_send[1] = gather_tops(t_send[0], t_row, "row", r)
-        t_cols = post(t_col, [(t_send.at[1], t_col.at[i], (0, off)) for i, off in enumerate(BEYOND)])
+        for group in t_rows:
+            group.wait_recv()
+        t_cols = post_tops(gather_tops(t_send[0], t_row, tp_row, tl_row, "row"), t_col, tp_col, tl_col, 1)
 
         m_cols.wait_recv()
         pl.semaphore_wait(far_sem, 2)
@@ -480,26 +501,30 @@
 
         row_weights = {a: side_weights(a) for a in (-1, 0, 1)}
 
-        for l in range(1, 5):
-
-            def blend(i, carry, l=l):
-                at = pl.multiple_of(i * 8, 8)
-                row = pl.multiple_of(ROW0[l] + i * 8, 8)
-                mask = None
-                for a in range(3):
-                    term = rowc[pl.ds(SPREAD_AT + 184 * a + row, 8), :][:, None, :] * inner[HALF[l]][a][None]
-                    mask = term if mask is None else mask + term
-                whole = jnp.sum(mask, axis=1)
-                inverse = jnp.where(whole > 0.0, 1.0 / jnp.where(whole > 0.0, whole, 1.0), 0.0)
-                for c in range(C):
-                    part = d[l][pl.ds(at, 8), V * c : V * c + V, :]
-                    planes[c, pl.ds(row, 8), :] = jnp.sum(part * mask, axis=1) * inverse
-                    if l == 1:
-                        part = copies_ref[pl.ds(at, 8), V * c : V * c + V, :]
-                        ones_ref[c, pl.ds(at, 8), :] = jnp.sum(part * row_weights[0][None], axis=1)
-                return carry
-
-            lax.fori_loop(0, ROWS[l] // 8, blend, 0)
+        def blend(i, l):
+            at, row = i * 8, ROW0[l] + i * 8
+            if not isinstance(i, int):
+                at, row = pl.multiple_of(at, 8), pl.multiple_of(row, 8)
+            mask = None
+            for a in range(3):
+                term = rowc[pl.ds(SPREAD_AT + 184 * a + row, 8), :][:, None, :] * inner[HALF[l]][a][None]
+                mask = term if mask is None else mask + term
+            whole = jnp.sum(mask, axis=1)
+            inverse = jnp.where(whole > 0.0, 1.0 / jnp.where(whole > 0.0, whole, 1.0), 0.0)
+            for c in range(C):
+                part = d[l][pl.ds(at, 8), V * c : V * c + V, :]
+                planes[c, pl.ds(row, 8), :] = jnp.sum(part * mask, axis=1) * inverse
+                if l == 1:
+                    part = copies_ref[pl.ds(at, 8), V * c : V * c + V, :]
+                    ones_ref[c, pl.ds(at, 8), :] = jnp.sum(part * row_weights[0][None], axis=1)
+
+        def blend_rest(i, carry, l):
+            blend(i, l)
+            return carry
+
+        for l, blocks in ((1, (0, 8, 9)), (2, (0, 4, 5)), (3, (0, 2, 3)), (4, (0, 1, 2))):
+            for i in blocks:
+                blend(i, l)
 
         for w in range(2):
             corners = [jnp.zeros((8, LANES), F32) for _ in range(2)]
@@ -522,6 +547,8 @@
         v_rims = post(v_recv, [(v_send.at[w], v_recv.at[w], (2 * w - 1, 0)) for w in range(2)])
         ends = [(i, 2 * (i // 2) - 1, 2 * (i % 2) - 1) for i in range(4)]
         c_rims = post(c_recv, [(c_send.at[i], c_recv.at[i], (a, b)) for i, a, b in ends])
+        for l, first, last in ((1, 1, 8), (2, 1, 4), (3, 1, 2)):
+            lax.fori_loop(first, last, lambda i, carry, l=l: blend_rest(i, carry, l), 0)
         for which in range(2):
             for g in range(SIDE_TILES):
                 tile = jnp.zeros((8, LANES), F32)
@@ -536,8 +563,17 @@
         for c in range(C):
             planes[c, 0:80] -= keep(ones_ref[c], 0, COPY0)
 
-        t_cols.wait_recv()
-        tops_all = gather_tops(t_send[1], t_col, "col", c_at)
+        own_weights = weights(own_mask)
+        for c in range(C):
+            total = None
+            for v in range(V):
+                term = x_ref[(v * C + c) * BLOCK : (v * C + c + 1) * BLOCK, :] * own_weights[v : v + 1, :]
+                total = term if total is None else total + term
+            xs_ref[c] = total
+
+        for group in t_cols:
+            group.wait_recv()
+        tops_all = gather_tops(t_send[1], t_col, tp_col, tl_col, "col")
         flat = [cols[FLAT_AT : FLAT_AT + LANES], cols[FLAT_AT + LANES : FLAT_AT + 2 * LANES]]
         images, mask = tops_all[0:24], tops_all[24:32]
         whole = jnp.sum(mask, axis=0, keepdims=True)
@@ -591,12 +627,17 @@
                 got = h_recv[which, i // 16] * flag
                 planes[c, row : row + 8] += keep(turn(got, first - 8 * u), first, first + 6)
 
+        def wide_dot(a, b):
+            return jnp.dot(a, b, precision=lax.Precision.HIGH, preferred_element_type=F32)
+
+        upper = wide_dot(jnp.concatenate([planes[c, 0:128] for c in range(C)], axis=0), cols[0:128])
+        lower = wide_dot(jnp.concatenate([planes[c, 128:192] for c in range(C)], axis=0), cols[128:256])
+        across = [jnp.concatenate([upper[128 * c : 128 * c + 128], lower[64 * c : 64 * c + 64]], axis=0) for c in range(C)]
+        total = wide_dot(
+            jnp.concatenate([rowc[0:128], rowc[128:256]], axis=1)[:, 0:192], jnp.concatenate(across, axis=1)
+        )
         for c in range(C):
-            upper = jnp.dot(rowc[0:128], planes[c, 0:128], precision=lax.Precision.HIGH, preferred_element_type=F32)
-            lower = jnp.dot(rowc[128:256, 0:64], planes[c, 128:192], precision=lax.Precision.HIGH, preferred_element_type=F32)
-            total = jnp.dot(upper, cols[0:128], precision=lax.Precision.HIGH, preferred_element_type=F32)
-            total = total + jnp.dot(lower, cols[128:256], precision=lax.Precision.HIGH, preferred_element_type=F32)
-            xs_ref[c] += total
+            xs_ref[c] += total[:, LANES * c : LANES * c + LANES]
 
         m_rows.wait_recv()
         means = m_send[1] + jnp.sum(m_row[...], axis=0)
@@ -633,8 +674,9 @@
         vmem(V, LANES),
         vmem(8, V, LANES),
         vmem(2, 32, LANES),
-        vmem(6, 32, LANES),
-        vmem(6, 32, LANES),
+        vmem(2, 16, LANES),
+        vmem(2, 8, LANES),
+        *[vmem(2, n, LANES) for n in (32, 16, 8, 32, 16, 8)],
         vmem(2, C, 2, 8, LANES),
         vmem(2, C, 2, 8, LANES),
         vmem(2, SIDE_TILES, 8, LANES),
@@ -644,8 +686,8 @@
         vmem(8 * V, LANES),
         vmem(V, BLOCK, LANES),
         pltpu.SemaphoreType.DMA((8,)),
-        pltpu.SemaphoreType.DMA((8,)),
-        pltpu.SemaphoreType.DMA((8,)),
+        pltpu.SemaphoreType.DMA((12,)),
+        pltpu.SemaphoreType.DMA((12,)),
         pltpu.SemaphoreType.REGULAR,
     ]
     return pl.pallas_call(

time: 31.1 us -> 30.1 us (0.968)
  Pallas kernels: 29 us -> 27.9 us
    pallas_call x1, Pallas kernels: 29 us -> 27.9 us  [local(): call(intersection_bits, seam_labels, planes, jnp.asarray(MATS), jnp.asarr...]
where the time goes in v3:
time: 30.1 us; the launch traced here: 29.9 us
  Pallas kernels  27.9 us (93%)
  between operations  1.3 us (4%)
  local copies, waits for them, and re-layouts  0.68 us (2%)
    pallas_call x1, Pallas kernels, local(): call(intersection_bits, seam_labels, planes, jnp.asarray(MATS), jnp.asarr...  27.9 us
    unnamed x1, local copies, waits for them, and re-layouts  0.68 us

profile of v3, /device:TPU:1, one launch (start us, length us, event | category | flops | bytes accessed | tf_op | source)
XLA Modules:
  0.0 29.9 jit_solution(15182656040158436880)
XLA Ops:
  1.3 27.9 %shard_map.64 = f32[3,128,128]{2,1,0:T(8,128)S(1)} custom-call(s32[1,1]{1,0:T(1,128)S(6)} %copy.8.bits_ref, s32[1,1]{1,0:T(1,128)S(6)} %copy.9.label_ref, f32[3072,128]{1,0:T(8,128)} %bitcast.1, bf16[5,1664,256]{2,1,0:T(8,128)(2,1)} %constant.6.clone.mats_hbm, f32[5,520,128]{2,1,0:T(8,128)} %constant.7.clone.cols_hbm, f32[5,944,128]{2,1,0:T(8,128)} %constant.8.clone.rows_hbm), custom_call_target="tpu_custom_call" | custom-call | tf_op jit(solution)/shard_map/pallas_call | solution.py:708
  29.2 0.7 %copy.10 = f32[3,128,128]{2,1,0:T(8,128)} copy(f32[3,128,128]{2,1,0:T(8,128)S(1)} %shard_map.64) | data formatting | bytes 393216

commit v4 on v3

--- a/solution.py
+++ b/solution.py
@@ -143,7 +143,13 @@
                 local[i, j + 1] += weight
         kron = np.einsum("ai,bj->ijab", local, local).reshape(w * w, v * v)
         flat[which, FLAT0[l] : FLAT0[l] + w * w, FLAT0[l - 1] : FLAT0[l - 1] + v * v] = kron
-    cols = [np.concatenate([part, flat[0], flat[1]]) for part in cols]
+    def flattened(part):
+        out = np.zeros((LANES, LANES))
+        for i in range(7):
+            out[7 * i : 7 * i + 7] = part[128 + LANE5 : 128 + LANE5 + 7]
+        return out
+
+    cols = [np.concatenate([part, flat[0], flat[1], flattened(part)]) for part in cols]
     return np.stack(mats), np.stack(cols).astype(np.float32), np.stack(rows).astype(np.float32)
 
 
@@ -191,7 +197,7 @@
     def kernel(bits_ref, label_ref, x_hbm, mats_hbm, cols_hbm, rows_hbm, out_ref, *scratch):
         (x_ref, mats, cols, rowc, s1, s2, s3, s4, s5, s6, s7, e1, e2, e3, e4, d1, d2, d3, d4, copies_ref, xs_ref,
          planes, ones_ref, m_send, m_col, m_row, mask_send, mask_recv, t_send, t_packed, t_last, t_row, tp_row, tl_row, t_col, tp_col, tl_col, v_send, v_recv, h_send,
-         h_recv, c_send, c_recv, lines_ref, w_ref, load_sem, send_sem, recv_sem, far_sem) = scratch
+         h_recv, c_send, c_recv, w_ref, load_sem, send_sem, recv_sem, far_sem) = scratch
         s = {1: s1, 2: s2, 3: s3, 4: s4, 5: s5, 6: s6, 7: s7}
         e = {1: e1, 2: e2, 3: e3, 4: e4}
         d = {1: d1, 2: d2, 3: d3, 4: d4}
@@ -275,7 +281,7 @@
         for l, n in ((1, 75), (2, 42), (3, 25), (4, 17)):
             d[l][n:] = jnp.zeros((ROWS[l] - n, 24, LANES), F32)
         copies_ref[75:] = jnp.zeros((5, 24, LANES), F32)
-        lines_ref[...] = jnp.zeros_like(lines_ref)
+        planes[:, ROW5:] = jnp.zeros((C, 192 - ROW5, LANES), F32)
 
         loads[0].wait()
         loads[1].wait()
@@ -571,37 +577,6 @@
                 total = term if total is None else total + term
             xs_ref[c] = total
 
-        for group in t_cols:
-            group.wait_recv()
-        tops_all = gather_tops(t_send[1], t_col, tp_col, tl_col, "col")
-        flat = [cols[FLAT_AT : FLAT_AT + LANES], cols[FLAT_AT + LANES : FLAT_AT + 2 * LANES]]
-        images, mask = tops_all[0:24], tops_all[24:32]
-        whole = jnp.sum(mask, axis=0, keepdims=True)
-        here = whole > 0.0
-        share = mask * jnp.where(here, 1.0 / jnp.where(here, whole, 1.0), 0.0)
-        finer = jnp.dot(images, flat[0] + flat[1], precision=lax.Precision.HIGHEST, preferred_element_type=F32)
-        detail = images - finer
-        blended = [jnp.sum(detail[V * c : V * c + V] * share, axis=0, keepdims=True) for c in range(C)]
-        balance = keep(jnp.sum(share, axis=0, keepdims=True) * (1.0 / V) - share, FLAT0[7], FLAT0[7] + 16)
-        chain = jnp.concatenate(blended + [jnp.zeros((8 - C, LANES), F32), balance], axis=0)
-        for which in range(2):
-            step = jnp.dot(chain, flat[which], precision=lax.Precision.HIGHEST, preferred_element_type=F32)
-            chain = chain + jnp.where(here, step, 0.0)
-
-        for c in range(C):
-            planes[c, ROW5 + 7 : ROW5 + 8] = jnp.zeros((1, LANES), F32)
-        for i in range(7):
-            line = keep(turn(chain, LANE5 - 7 * i), LANE5, LANE5 + 7)
-            for c in range(C):
-                planes[c, ROW5 + i : ROW5 + i + 1] = line[c : c + 1]
-            for v in range(V):
-                lines_ref[8 * v + i : 8 * v + i + 1] = line[8 + v : 9 + v]
-        wide = jnp.dot(lines_ref[...], cols[128:256], precision=lax.Precision.HIGH, preferred_element_type=F32)
-        for v in range(V):
-            w_ref[v] = jnp.dot(
-                rowc[128:256, 56:64], wide[8 * v : 8 * v + 8], precision=lax.Precision.HIGH, preferred_element_type=F32
-            )
-
         v_rims.wait_recv()
         c_rims.wait_recv()
         h_rims.wait_recv()
@@ -638,6 +613,33 @@
         )
         for c in range(C):
             xs_ref[c] += total[:, LANES * c : LANES * c + LANES]
+
+        for group in t_cols:
+            group.wait_recv()
+        tops_all = gather_tops(t_send[1], t_col, tp_col, tl_col, "col")
+        flat = [cols[FLAT_AT : FLAT_AT + LANES], cols[FLAT_AT + LANES : FLAT_AT + 2 * LANES]]
+        images, mask = tops_all[0:24], tops_all[24:32]
+        whole = jnp.sum(mask, axis=0, keepdims=True)
+        here = whole > 0.0
+        share = mask * jnp.where(here, 1.0 / jnp.where(here, whole, 1.0), 0.0)
+        finer = jnp.dot(images, flat[0] + flat[1], precision=lax.Precision.HIGHEST, preferred_element_type=F32)
+        detail = images - finer
+        blended = [jnp.sum(detail[V * c : V * c + V] * share, axis=0, keepdims=True) for c in range(C)]
+        balance = keep(jnp.sum(share, axis=0, keepdims=True) * (1.0 / V) - share, FLAT0[7], FLAT0[7] + 16)
+        chain = jnp.concatenate(blended + [jnp.zeros((8 - C, LANES), F32), balance], axis=0)
+        for which in range(2):
+            step = jnp.dot(chain, flat[which], precision=lax.Precision.HIGHEST, preferred_element_type=F32)
+            chain = chain + jnp.where(here, step, 0.0)
+
+        diagonal = jnp.logical_and(lane // 7 == view, lane < 49)
+        spread = [jnp.where(diagonal, jnp.broadcast_to(chain[u : u + 1], (8, LANES)), 0.0) for u in (*range(C), *range(8, 16))]
+        wide = wide_dot(jnp.concatenate(spread, axis=0), cols[FLAT_AT + 256 : FLAT_AT + 384])
+        each = [wide[8 * u : 8 * u + 8] for u in range(C + V)]
+        total = wide_dot(rowc[128:256, 56:64], jnp.concatenate(each, axis=1))
+        for c in range(C):
+            xs_ref[c] += total[:, LANES * c : LANES * c + LANES]
+        for v in range(V):
+            w_ref[v] = total[:, LANES * (C + v) : LANES * (C + v) + LANES]
 
         m_rows.wait_recv()
         means = m_send[1] + jnp.sum(m_row[...], axis=0)
@@ -683,7 +685,6 @@
         vmem(2, SIDE_TILES, 8, LANES),
         vmem(4, 8, LANES),
         vmem(4, 8, LANES),
-        vmem(8 * V, LANES),
         vmem(V, BLOCK, LANES),
         pltpu.SemaphoreType.DMA((8,)),
         pltpu.SemaphoreType.DMA((12,)),

time: 30.1 us -> 30 us (level)
  no operation moved by 1% of the time
where the time goes in v4:
time: 30 us; the launch traced here: 29.8 us
  Pallas kernels  27.8 us (93%)
  between operations  1.3 us (4%)
  local copies, waits for them, and re-layouts  0.68 us (2%)
    pallas_call x1, Pallas kernels, local(): call(intersection_bits, seam_labels, planes, jnp.asarray(MATS), jnp.asarr...  27.8 us
    unnamed x1, local copies, waits for them, and re-layouts  0.68 us

profile of v4, /device:TPU:1, one launch (start us, length us, event | category | flops | bytes accessed | tf_op | source)
XLA Modules:
  0.0 29.8 jit_solution(5763251478896677618)
XLA Ops:
  1.3 27.8 %shard_map.64 = f32[3,128,128]{2,1,0:T(8,128)S(1)} custom-call(s32[1,1]{1,0:T(1,128)S(6)} %copy.8.bits_ref, s32[1,1]{1,0:T(1,128)S(6)} %copy.9.label_ref, f32[3072,128]{1,0:T(8,128)} %bitcast.1, bf16[5,1664,256]{2,1,0:T(8,128)(2,1)} %constant.6.clone.mats_hbm, f32[5,648,128]{2,1,0:T(8,128)} %constant.7.clone.cols_hbm, f32[5,944,128]{2,1,0:T(8,128)} %constant.8.clone.rows_hbm), custom_call_target="tpu_custom_call" | custom-call | tf_op jit(solution)/shard_map/pallas_call | solution.py:709
  29.1 0.7 %copy.10 = f32[3,128,128]{2,1,0:T(8,128)} copy(f32[3,128,128]{2,1,0:T(8,128)S(1)} %shard_map.64) | data formatting | bytes 393216
